TPU v7x, 32 devices: a whole 2x2x4 slice. The times are simulated.
32 devices in a mesh: dp: 16 (over z, x, core), tensor: 2 (over y).
Axes of the slice: x: 2, y: 2, z: 4, core: 2. Of those that a mesh axis runs over, the one named last changes fastest.
Arguments:
- tokens: bfloat16 [4096, 1024], P('dp'), may hold values from -6 to 6
- cotangent: bfloat16 [4096, 1024], P('dp'), may hold values from -6 to 6
- lengths: int32 [4], replicated, may hold values from 1 to 32, 64 in all
- norm_gains: bfloat16 [2, 1024], replicated, may hold values from 0.5 to 1.5
- query_key_weight: bfloat16 [1024, 2, 1024], P('dp', None, 'tensor'), may hold values from -0.1875 to 0.1875
- value_gate_weight: bfloat16 [1024, 2, 2048], P('dp', None, 'tensor'), may hold values from -0.1875 to 0.1875
- decay_beta_weight: bfloat16 [1024, 2, 8], P('dp', None, 'tensor'), may hold values from -0.1875 to 0.1875
- conv_query_key: bfloat16 [4, 2, 1024], P(None, None, 'tensor'), may hold values from -3 to 3
- conv_value: bfloat16 [4, 2048], P(None, 'tensor'), may hold values from -3 to 3
- decay_log: float32 [8], P('tensor'), may hold values from -6 to -1.5
- decay_bias: float32 [8], P('tensor'), may hold values from -2 to 1
- output_gain: bfloat16 [256], replicated, may hold values from 0.5 to 1.5
- out_weight: bfloat16 [1024, 2048], P('dp', 'tensor'), may hold values from -0.25 to 0.25
- gate_up_weight: bfloat16 [1024, 2, 2816], P('dp', None, 'tensor'), may hold values from -0.1875 to 0.1875
- down_weight: bfloat16 [1024, 2816], P('dp', 'tensor'), may hold values from -0.21875 to 0.21875
Outputs:
- output: bfloat16 [4096, 1024], P('dp')
- grad_tokens: float32 [4096, 1024], P('dp')
- grad_norm_gains: float32 [2, 1024], replicated
- grad_query_key: float32 [1024, 2, 1024], P('dp', None, 'tensor')
- grad_value_gate: float32 [1024, 2, 2048], P('dp', None, 'tensor')
- grad_decay_beta: float32 [1024, 2, 8], P('dp', None, 'tensor')
- grad_conv_query_key: float32 [4, 2, 1024], P(None, None, 'tensor')
- grad_conv_value: float32 [4, 2048], P(None, 'tensor')
- grad_decay_log: float32 [8], P('tensor')
- grad_decay_bias: float32 [8], P('tensor')
- grad_output_gain: float32 [256], replicated
- grad_out_weight: float32 [1024, 2048], P('dp', 'tensor')
- grad_gate_up: float32 [1024, 2, 2816], P('dp', None, 'tensor')
- grad_down: float32 [1024, 2816], P('dp', 'tensor')
Inputs may be any that keep to these rules, and one draw needn't show every extreme that they name: Each sequence's length in blocks of 64 tokens; the lengths sum to 64 and the longest is exactly 32.
All inputs are finite; a program needn't handle non-finite values.
Results may differ from a plain program's by a relative error of at most 0.013.
The roundings to bfloat16 on the way count: a program that leaves them out, or rounds other values in their place, can miss the bound.
Values may be sent and summed in bfloat16 or wider, within the bound.
A program may use at most 448 MiB of HBM per device.

v0:
```python
import jax
import jax.numpy as jnp
from jax import lax
from jax.sharding import PartitionSpec as P

DK = 128
DV = 256
GROUP = 64


high_accuracy_mode = lax.Precision.HIGHEST


def shifted(block, axis, distance):
    devices = range(lax.axis_size(axis))
    route = [(i - distance, i) for i in devices if i - distance in devices]
    return lax.ppermute(block, axis, route)


def carried_in(value, axis, join, neutral, backward):
    count, mine = (lax.axis_size(axis), lax.axis_index(axis))
    pieces = jax.tree.map(lambda part: lax.all_gather(part, axis), value)
    if backward:
        pieces = jax.tree.map(lambda part: part[::-1], pieces)
        mine = count - 1 - mine
    so_far = jax.tree.map(
        lambda part, zero: jnp.full_like(part, 0) + jnp.asarray(zero, part.dtype), value, neutral
    )

    def lap(position, so_far):
        longer = join(so_far, jax.tree.map(lambda part: part[position], pieces))
        return jax.tree.map(lambda new, old: jnp.where(position < mine, new, old), longer, so_far)

    return lax.fori_loop(0, count - 1, lap, so_far)


def round_low(values):
    return lax.optimization_barrier(values.astype(jnp.bfloat16)).astype(jnp.float32)


def unit_rows(values, epsilon):
    return values * lax.rsqrt(jnp.mean(values * values, axis=-1, keepdims=True) + epsilon)


def unit_sphere(values):
    return values * lax.rsqrt(jnp.sum(values * values, axis=-1, keepdims=True) + 1e-06)


def norm_back(grad_unit, unit_value, scale_rows):
    return scale_rows * (
        grad_unit - unit_value * jnp.mean(grad_unit * unit_value, axis=-1, keepdims=True)
    )


def to_blocks(rows_data, size):
    count = rows_data.shape[0] // size
    return rows_data.reshape(count, size, rows_data.shape[1], -1).transpose(0, 2, 1, 3)


def from_blocks(blocked):
    return blocked.transpose(0, 2, 1, 3).reshape(-1, blocked.shape[1], blocked.shape[3])


def group_parts(key_rows, value_rows, beta_rows, log_decay):
    length = key_rows.shape[1]
    running_decay_total = jnp.cumsum(log_decay, axis=-1)
    row_index = lax.broadcasted_iota(jnp.int32, (length, length), 0)
    col_index = lax.broadcasted_iota(jnp.int32, (length, length), 1)
    spread = running_decay_total[:, :, None] - running_decay_total[:, None, :]
    ratio = jnp.where(row_index >= col_index, jnp.exp(jnp.minimum(spread, 0.0)), 0.0)
    strict = jnp.where(row_index > col_index, ratio, 0.0)
    inner = jnp.einsum("hck,hdk->hcd", key_rows, key_rows, precision=high_accuracy_mode)
    system = jnp.eye(length, dtype=jnp.float32) + beta_rows[:, :, None] * strict * inner
    decay = jnp.exp(running_decay_total)
    right = jnp.concatenate(
        [beta_rows[:, :, None] * value_rows, (beta_rows * decay)[:, :, None] * key_rows], axis=-1
    )
    solved = lax.linalg.triangular_solve(system, right, left_side=True, lower=True)
    vwidth = value_rows.shape[-1]
    return (running_decay_total, ratio, decay, solved[..., :vwidth], solved[..., vwidth:])


def group_out(
    state_sequence, query_rows_local, key_rows, value_rows, beta_rows, log_decay, keep_flag
):
    state_sequence = state_sequence * keep_flag
    running_decay_total, ratio, decay, solved_value_rows, solved_weight_rows = group_parts(
        key_rows, value_rows, beta_rows, log_decay
    )
    newly_written_state = solved_value_rows - jnp.einsum(
        "pel,pln->pen", solved_weight_rows, state_sequence, precision=high_accuracy_mode
    )
    scores = (
        jnp.einsum("hck,hdk->hcd", query_rows_local, key_rows, precision=high_accuracy_mode) * ratio
    )
    carried_over_state = jnp.einsum(
        "pel,pln->pen", query_rows_local, state_sequence, precision=high_accuracy_mode
    )
    result = (
        decay[:, :, None] * carried_over_state
        + jnp.einsum("hcd,hdv->hcv", scores, newly_written_state, precision=high_accuracy_mode)
    ) * query_rows_local.shape[-1] ** (-0.5)
    trailing_rows = (
        jnp.exp(running_decay_total[:, -1:] - running_decay_total)[:, :, None] * key_rows
    )
    refreshed_state = jnp.exp(running_decay_total[:, -1])[
        :, None, None
    ] * state_sequence + jnp.einsum(
        "ypt,ypr->ytr", trailing_rows, newly_written_state, precision=high_accuracy_mode
    )
    return (refreshed_state, result)


def transition(key_rows, value_rows, beta_rows, log_decay, keep_flags):
    head_count, length, key_size = (key_rows.shape[1], key_rows.shape[2], key_rows.shape[3])
    identity = jnp.broadcast_to(
        jnp.eye(key_size, dtype=jnp.float32), (head_count, key_size, key_size)
    )

    def absorb(carry, pieces):
        mat_a, mat_b = carry
        block_k, block_v, block_b, block_g, keep_flag = pieces
        running_decay_total, ratio, decay, solved_value_rows, solved_weight_rows = group_parts(
            block_k, block_v, block_b, block_g
        )
        trailing_rows = (
            jnp.exp(running_decay_total[:, -1:] - running_decay_total)[:, :, None] * block_k
        )
        step_a = keep_flag * (
            jnp.exp(running_decay_total[:, -1])[:, None, None] * identity
            - jnp.einsum(
                "hck,hcj->hkj", trailing_rows, solved_weight_rows, precision=high_accuracy_mode
            )
        )
        second_step_matrix = jnp.einsum(
            "ypt,ypr->ytr", trailing_rows, solved_value_rows, precision=high_accuracy_mode
        )
        return (
            (
                jnp.einsum("hij,hjk->hik", step_a, mat_a, precision=high_accuracy_mode),
                jnp.einsum("hij,hjv->hiv", step_a, mat_b, precision=high_accuracy_mode)
                + second_step_matrix,
            ),
            None,
        )

    start = (identity, jnp.zeros((head_count, key_size, value_rows.shape[3]), jnp.float32))
    final, unused = lax.scan(
        absorb, start, (key_rows, value_rows, beta_rows, log_decay, keep_flags)
    )
    return final


def local_outputs(
    state_sequence, query_rows_local, key_rows, value_rows, beta_rows, log_decay, keep_flags
):

    def advance(carry, pieces):
        return group_out(carry, *pieces)

    unused, blocked = lax.scan(
        advance,
        state_sequence,
        (query_rows_local, key_rows, value_rows, beta_rows, log_decay, keep_flags),
    )
    return blocked


def compose(earlier, later):
    return (
        jnp.einsum("hij,hjk->hik", later[0], earlier[0], precision=high_accuracy_mode),
        jnp.einsum("hij,hjv->hiv", later[0], earlier[1], precision=high_accuracy_mode) + later[1],
    )


def front(extended, proj_ab, conv_taps, decay_log, decay_bias, inside):
    row_count = proj_ab.shape[0]
    head_count = decay_log.shape[0]
    taps = conv_taps.shape[0]
    conv_sum = conv_taps[0] * extended[0:row_count] * inside[0]
    for tap_index in range(1, taps):
        conv_sum = (
            conv_sum
            + conv_taps[tap_index] * extended[tap_index : tap_index + row_count] * inside[tap_index]
        )
    activated = jax.nn.silu(conv_sum)
    width_k = head_count * DK
    query_rows_local = unit_sphere(activated[:, :width_k].reshape(row_count, head_count, DK))
    key_rows = unit_sphere(activated[:, width_k : 2 * width_k].reshape(row_count, head_count, DK))
    value_rows = activated[:, 2 * width_k :].reshape(row_count, head_count, DV)
    beta_rows = jax.nn.sigmoid(proj_ab[:, head_count:])
    log_decay = -jnp.exp(decay_log) * jax.nn.softplus(proj_ab[:, :head_count] + decay_bias)
    return (query_rows_local, key_rows, value_rows, beta_rows, log_decay)


def gated_output(heads_out, gate_raw, output_gain):
    gate_heads = gate_raw.reshape(heads_out.shape)
    return (unit_rows(heads_out, 1e-05) * output_gain * jax.nn.silu(gate_heads)).reshape(
        gate_raw.shape
    )


def contract_rows(left, right):
    return lax.dot_general(
        left, right, (((0,), (0,)), ((), ())), preferred_element_type=jnp.float32
    )


def contract_cols(left, right):
    return lax.dot_general(
        left, right, (((1,), (1,)), ((), ())), preferred_element_type=jnp.float32
    )


def local(
    tokens,
    cotangent,
    lengths,
    norm_gains,
    query_key_weight,
    value_gate_weight,
    decay_beta_weight,
    conv_query_key,
    conv_value,
    decay_log,
    decay_bias,
    output_gain,
    out_weight,
    gate_up_weight,
    down_weight,
):
    row_count, width = tokens.shape
    head_count = decay_log.shape[0]
    width_k = head_count * DK
    width_v = head_count * DV
    taps = conv_query_key.shape[0]
    rim_rows = taps - 1
    first_row = lax.axis_index("dp") * row_count
    positions = first_row + lax.broadcasted_iota(jnp.int32, (row_count,), 0)
    seq_starts = (jnp.cumsum(lengths) - lengths) * GROUP
    seg_first = jnp.max(
        jnp.where(seq_starts[None, :] <= positions[:, None], seq_starts[None, :], 0), axis=1
    )
    block_first = positions[::GROUP]
    keep_flags = 1.0 - jnp.any(seq_starts[None, :] == block_first[:, None], axis=1).astype(
        jnp.float32
    )
    inside = jnp.stack(
        [
            (positions - (rim_rows - tap_index) >= seg_first).astype(jnp.float32)[:, None]
            for tap_index in range(taps)
        ]
    )
    gains = norm_gains.astype(jnp.float32)
    inputs = tokens.astype(jnp.float32)
    scale_one = lax.rsqrt(jnp.mean(inputs * inputs, axis=-1, keepdims=True) + 1e-06)
    unit_one = inputs * scale_one
    normed = (unit_one * gains[0]).astype(jnp.bfloat16)
    full_qk, full_vg, full_ab, full_out = (
        lax.all_gather(query_key_weight, "dp", axis=0, tiled=True),
        lax.all_gather(value_gate_weight, "dp", axis=0, tiled=True),
        lax.all_gather(decay_beta_weight, "dp", axis=0, tiled=True),
        lax.all_gather(out_weight, "dp", axis=0, tiled=True),
    )
    proj_qk = jnp.dot(
        normed, full_qk.reshape(width, 2 * width_k), preferred_element_type=jnp.float32
    )
    proj_vg = jnp.dot(
        normed, full_vg.reshape(width, 2 * width_v), preferred_element_type=jnp.float32
    )
    proj_ab = jnp.dot(
        normed, full_ab.reshape(width, 2 * head_count), preferred_element_type=jnp.float32
    )
    pre_conv = jnp.concatenate([proj_qk, proj_vg[:, :width_v]], axis=1).astype(jnp.bfloat16)
    gate_raw = proj_vg[:, width_v:]
    rim = shifted(pre_conv[row_count - rim_rows :], "dp", 1)
    extended = jnp.concatenate([rim, pre_conv], axis=0).astype(jnp.float32)
    conv_taps = jnp.concatenate(
        [conv_query_key.reshape(taps, 2 * width_k), conv_value], axis=1
    ).astype(jnp.float32)

    def front_piece(ext_rows, ab_rows, tap_rows, log_rate, rate_bias):
        return front(ext_rows, ab_rows, tap_rows, log_rate, rate_bias, inside)

    fronted, front_back = jax.vjp(front_piece, extended, proj_ab, conv_taps, decay_log, decay_bias)
    query_rows_local, key_rows, value_rows, beta_rows, log_decay = fronted
    block_q = to_blocks(round_low(query_rows_local), GROUP)
    block_k = to_blocks(round_low(key_rows), GROUP)
    block_v = to_blocks(round_low(value_rows), GROUP)
    block_b = to_blocks(beta_rows[:, :, None], GROUP)[..., 0]
    block_g = to_blocks(log_decay[:, :, None], GROUP)[..., 0]

    def transition_piece(keys_in, values_in, betas_in, decays_in):
        return transition(keys_in, values_in, betas_in, decays_in, keep_flags)

    (trans_a, trans_b), trans_back = jax.vjp(transition_piece, block_k, block_v, block_b, block_g)
    eye_stack = jnp.broadcast_to(jnp.eye(DK, dtype=jnp.float32), (head_count, DK, DK))
    zero_state = jnp.zeros((head_count, DK, DV), jnp.float32)
    prefix_a, entering_state = carried_in(
        (trans_a, trans_b), "dp", compose, (eye_stack, zero_state), False
    )

    def output_piece(state_sequence, queries_in, keys_in, values_in, betas_in, decays_in):
        return local_outputs(
            state_sequence, queries_in, keys_in, values_in, betas_in, decays_in, keep_flags
        )

    block_out, out_back = jax.vjp(
        output_piece, entering_state, block_q, block_k, block_v, block_b, block_g
    )
    heads_out = from_blocks(block_out)
    gated, gated_back = jax.vjp(gated_output, heads_out, gate_raw, output_gain.astype(jnp.float32))
    gated_low = gated.astype(jnp.bfloat16)
    mixed_sum = lax.psum(contract_cols(gated_low, full_out), "tensor")
    residual = inputs + mixed_sum
    scale_two = lax.rsqrt(jnp.mean(residual * residual, axis=-1, keepdims=True) + 1e-06)
    unit_two = residual * scale_two
    normed_two = (unit_two * gains[1]).astype(jnp.bfloat16)
    full_gu, full_down = (
        lax.all_gather(gate_up_weight, "dp", axis=0, tiled=True),
        lax.all_gather(down_weight, "dp", axis=0, tiled=True),
    )
    ff_local = full_down.shape[1]
    matrix_gu = full_gu.reshape(width, 2 * ff_local)
    up_gate = jnp.dot(normed_two, matrix_gu, preferred_element_type=jnp.float32)
    gate_two = up_gate[:, :ff_local]
    up_two = up_gate[:, ff_local:]
    hidden = (jax.nn.silu(gate_two) * up_two).astype(jnp.bfloat16)
    mlp_total = lax.psum(contract_cols(hidden, full_down).astype(jnp.bfloat16), "tensor").astype(
        jnp.float32
    )
    output = (residual + mlp_total).astype(jnp.bfloat16)
    grad_out = cotangent.astype(jnp.float32)
    grad_hidden = jnp.dot(cotangent, full_down, preferred_element_type=jnp.float32)
    grad_down = contract_rows(cotangent, hidden)
    sigma_two = jax.nn.sigmoid(gate_two)
    grad_gate_two = grad_hidden * up_two * sigma_two * (1.0 + gate_two * (1.0 - sigma_two))
    grad_up_two = grad_hidden * gate_two * sigma_two
    grad_gu_low = jnp.concatenate([grad_gate_two, grad_up_two], axis=1).astype(jnp.bfloat16)
    grad_gate_up = contract_rows(normed_two, grad_gu_low).reshape(full_gu.shape)
    grad_normed_two_part = contract_cols(grad_gu_low, matrix_gu)
    grad_normed_two = lax.psum(grad_normed_two_part, "tensor")
    gain_two_grad = jnp.sum(grad_normed_two * unit_two, axis=0)
    grad_residual = grad_out + norm_back(grad_normed_two * gains[1], unit_two, scale_two)
    grad_res_low = grad_residual.astype(jnp.bfloat16)
    grad_gated = jnp.dot(grad_res_low, full_out, preferred_element_type=jnp.float32)
    grad_out_weight = contract_rows(grad_res_low, gated_low)
    grad_heads, grad_gate_raw, grad_gain_part = gated_back(grad_gated)
    grad_state_in, grad_bq, grad_bk, grad_bv, grad_bb, grad_bg = out_back(
        to_blocks(grad_heads, GROUP)
    )
    flipped = jnp.swapaxes(trans_a, 1, 2)
    prefix_flip, gradient_final_state = carried_in(
        (flipped, grad_state_in), "dp", compose, (eye_stack, zero_state), True
    )
    gradient_transition_left = jnp.einsum(
        "xpt,xct->xpc", gradient_final_state, entering_state, precision=high_accuracy_mode
    )
    extra_k, extra_v, extra_b, extra_g = trans_back(
        (gradient_transition_left, gradient_final_state)
    )
    grad_queries = from_blocks(grad_bq)
    grad_keys = from_blocks(grad_bk + extra_k)
    grad_values = from_blocks(grad_bv + extra_v)
    grad_betas = from_blocks((grad_bb + extra_b)[..., None])[..., 0]
    grad_decays = from_blocks((grad_bg + extra_g)[..., None])[..., 0]
    grad_ext, grad_ab, grad_taps, grad_decay_log, grad_decay_bias = front_back(
        (grad_queries, grad_keys, grad_values, grad_betas, grad_decays)
    )
    rim_grad = shifted(grad_ext[:rim_rows], "dp", -1)
    grad_pre = grad_ext[rim_rows:] + jnp.concatenate(
        [jnp.zeros((row_count - rim_rows, grad_ext.shape[1]), jnp.float32), rim_grad], axis=0
    )
    grad_pre_low = grad_pre.astype(jnp.bfloat16)
    grad_qk_low = grad_pre_low[:, : 2 * width_k]
    grad_vg_low = jnp.concatenate(
        [grad_pre_low[:, 2 * width_k :], grad_gate_raw.astype(jnp.bfloat16)], axis=1
    )
    grad_ab_low = grad_ab.astype(jnp.bfloat16)
    grad_query_key = contract_rows(normed, grad_qk_low).reshape(full_qk.shape)
    grad_value_gate = contract_rows(normed, grad_vg_low).reshape(full_vg.shape)
    grad_decay_beta = contract_rows(normed, grad_ab_low).reshape(full_ab.shape)
    grad_normed_part = (
        contract_cols(grad_qk_low, full_qk.reshape(width, 2 * width_k))
        + contract_cols(grad_vg_low, full_vg.reshape(width, 2 * width_v))
        + contract_cols(grad_ab_low, full_ab.reshape(width, 2 * head_count))
    )
    grad_normed, grad_gain_out = (
        lax.psum(grad_normed_part.astype(jnp.bfloat16), "tensor").astype(jnp.float32),
        lax.psum(grad_gain_part.astype(jnp.bfloat16), "tensor").astype(jnp.float32),
    )
    gain_one_grad = jnp.sum(grad_normed * unit_one, axis=0)
    grad_tokens = grad_residual + norm_back(grad_normed * gains[0], unit_one, scale_one)
    share_qk, share_vg, share_ab, share_out, share_gu, share_down = (
        lax.psum_scatter(grad_query_key, "dp", scatter_dimension=0, tiled=True),
        lax.psum_scatter(grad_value_gate, "dp", scatter_dimension=0, tiled=True),
        lax.psum_scatter(grad_decay_beta, "dp", scatter_dimension=0, tiled=True),
        lax.psum_scatter(grad_out_weight, "dp", scatter_dimension=0, tiled=True),
        lax.psum_scatter(grad_gate_up, "dp", scatter_dimension=0, tiled=True),
        lax.psum_scatter(grad_down, "dp", scatter_dimension=0, tiled=True),
    )
    small = lax.psum(
        (
            jnp.stack([gain_one_grad, gain_two_grad]),
            grad_taps[:, : 2 * width_k].reshape(conv_query_key.shape),
            grad_taps[:, 2 * width_k :],
            grad_decay_log,
            grad_decay_bias,
            grad_gain_out,
        ),
        "dp",
    )
    return (
        output,
        grad_tokens,
        small[0],
        share_qk,
        share_vg,
        share_ab,
        small[1],
        small[2],
        small[3],
        small[4],
        small[5],
        share_out,
        share_gu,
        share_down,
    )


def solution(mesh):
    in_specs = (
        P("dp", None),
        P("dp", None),
        P(),
        P(),
        P("dp", None, "tensor"),
        P("dp", None, "tensor"),
        P("dp", None, "tensor"),
        P(None, None, "tensor"),
        P(None, "tensor"),
        P("tensor"),
        P("tensor"),
        P(),
        P("dp", "tensor"),
        P("dp", None, "tensor"),
        P("dp", "tensor"),
    )
    out_specs = (
        P("dp", None),
        P("dp", None),
        P(),
        P("dp", None, "tensor"),
        P("dp", None, "tensor"),
        P("dp", None, "tensor"),
        P(None, None, "tensor"),
        P(None, "tensor"),
        P("tensor"),
        P("tensor"),
        P(),
        P("dp", "tensor"),
        P("dp", None, "tensor"),
        P("dp", "tensor"),
    )
    return jax.shard_map(local, mesh=mesh, in_specs=in_specs, out_specs=out_specs, check_vma=False)
```

profile of v0, /device:TPU:0, one launch (start us, length us, event | category | flops | bytes accessed | tf_op | source)
XLA Modules:
  0.0 2205.2 jit_solution(5562624885982228391)
XLA Ops:
  9.7 24.9 %all_gather.42 = bf16[1024,2,4]{2,1,0:T(2,128)(2,1)S(1)} all-gather(bf16[64,2,4]{2,1,0:T(2,128)(2,1)S(1)} %copy.461), channel_id=1, replica_groups=mesh['dp'=16,'tensor'=2] {'dp'}, dimensions={0}, use_global_device_ids=true | all-gather | bytes 17408 | tf_op jit(solution)/shard_map/all_gather | solution.py:262
  39.2 15.5 all-gather.14.cloned.1.call-done
  57.6 48.7 %all-gather.16.cloned.1.call-done = bf16[1024,2,1024]{2,1,0:T(2,128)(2,1)} async-done(((bf16[64,2,1024]{2,1,0:T(2,128)(2,1)}), bf16[1024,2,1024]{2,1,0:T(2,128)(2,1)}) %all-gather.16.cloned.1.call-update) | async-done | bytes 4194320 | tf_op jit(solution)/shard_map/all_gather | solution.py:261
  147.4 174.7 %while.208 = (s32[]{:T(128)}, f32[4,128,128]{2,1,0:T(8,128)}, f32[4,128,256]{2,1,0:T(8,128)}, f32[4,4,64,64]{3,2,1,0:T(8,128)}, f32[4,4,64,64]{3,2,1,0:T(8,128)}...) while((s32[]{:T(128)}, f32[4,128,128]{2,1,0:T(8,128)}, ...), condition=%wide.region_7.9_spmd.clone.clone, body=%wide.region_5.8_spmd.clone.clone.sunk | while | flops 554955776 | bytes 11438636 | solution.py:148
  154.5 20.3 custom-call.31
  196.6 20.3 custom-call.31
  240.8 20.3 custom-call.31
  285.0 20.3 custom-call.31
  327.5 47.0 %all-gather.24.cloned.1.call-done = f32[64,128,128]{2,1,0:T(8,128)} async-done(((f32[4,128,128]{2,1,0:T(8,128)}), f32[64,128,128]{2,1,0:T(8,128)}) %all-gather.24.cloned.1.call-update) | async-done | bytes 4194320 | tf_op jit(solution)/shard_map/all_gather | solution.py:22
  374.5 76.0 %all-gather.26.cloned.1.call-done = f32[64,128,256]{2,1,0:T(8,128)} async-done(((f32[4,128,256]{2,1,0:T(8,128)}), f32[64,128,256]{2,1,0:T(8,128)}) %all-gather.26.cloned.1.call-update) | async-done | bytes 8388624 | tf_op jit(solution)/shard_map/all_gather | solution.py:22
  450.5 53.8 %while.206 = (s32[]{:T(128)}, f32[4,128,256]{2,1,0:T(8,128)}, s32[]{:T(128)}, f32[16,4,128,128]{3,2,1,0:T(8,128)}, f32[16,4,128,256]{3,2,1,0:T(8,128)}, /*index=5*/s32[]{:T(128)}, s32[]{:T(128)}) while((s32[]{:T(128)}, f32[4,128,256]{2,1,0:T(8,128)}, s32[]{:T(128)}, f32[16,4,128,128]{3,2,1,0:T(8,128)}, ...), condition=%wide.region_9.11_spmd.clone, body=%wide.region_8.10_spmd.clone.sunk | while | flops 201850880 | bytes 3410535 | solution.py:34
  525.5 180.4 %while.204 = (s32[]{:T(128)}, f32[4,128,256]{2,1,0:T(8,128)S(1)}, f32[4,4,64,256]{3,2,1,0:T(8,128)}, f32[4,4,64,64]{3,2,1,0:T(8,128)}, f32[4,4,64,64]{3,2,1,0:T(...) while((s32[]{:T(128)}, f32[4,128,256]{2,1,0:T(8,128)S(1)}, ...), condition=%wide.region_13.15_spmd.clone.clone, body=%wide.region_11.14_spmd.clone.clone.sunk | while | flops 479966208 | bytes 11845713 | solution.py:161
  535.9 21.0 custom-call.29
  581.0 21.0 custom-call.29
  626.1 21.0 custom-call.29
  671.2 21.0 custom-call.29
  716.5 6.2 copy.590
  722.7 31.5 %all-reduce.33.cloned.1.call-done = f32[256,1024]{1,0:T(8,128)} async-done(((f32[256,1024]{1,0:T(8,128)}), f32[256,1024]{1,0:T(8,128)}) %all-reduce.33.cloned.1.call-update) | async-done | bytes 1048592 | tf_op jit(solution)/shard_map/psum | solution.py:314
  756.6 6.0 fusion.355
  762.5 38.5 %all-gather.22.cloned.1.call-done = bf16[1024,1408]{1,0:T(8,128)(2,1)} async-done(((bf16[64,1408]{1,0:T(8,128)(2,1)}), bf16[1024,1408]{1,0:T(8,128)(2,1)}) %all-gather.22.cloned.1.call-update) | async-done | bytes 2883600 | tf_op jit(solution)/shard_map/all_gather | solution.py:321
  801.1 5.0 multiply_convert_fusion.1
  812.0 36.4 %all-reduce.35.cloned.1.call-done = f32[256,1024]{1,0:T(8,128)} async-done(((f32[256,1024]{1,0:T(8,128)}), f32[256,1024]{1,0:T(8,128)}) %all-reduce.35.cloned.1.call-update) | async-done | bytes 1048592 | tf_op jit(solution)/shard_map/psum | solution.py:342
  871.9 218.9 %while.209 = (s32[]{:T(128)}, f32[4,128,256]{2,1,0:T(8,128)S(1)}, f32[4,4,64,128]{3,2,1,0:T(8,128)}, f32[4,4,64,128]{3,2,0,1:T(8,128)}, f32[4,4,64,256]{3,2,1,0:...) while((s32[]{:T(128)}, f32[4,128,256]{2,1,0:T(8,128)S(1)}, ...), condition=%wide.region_32.36_spmd.clone.clone, body=%wide.region_21.35_spmd.clone.clone.sunk | while | flops 971938048 | bytes 25921988 | solution.py:161
  880.4 21.0 custom-call.32
  935.1 21.0 custom-call.32
  989.9 21.0 custom-call.32
  1044.6 21.0 custom-call.32
  1096.3 4.7 rev.6
  1107.6 59.0 %all-gather.30.cloned.1.call-done = f32[64,128,256]{2,1,0:T(8,128)} async-done(((f32[4,128,256]{2,1,0:T(8,128)}), f32[64,128,256]{2,1,0:T(8,128)}) %all-gather.30.cloned.1.call-update) | async-done | bytes 8388624 | tf_op jit(solution)/shard_map/all_gather | solution.py:22
  1166.6 7.7 rev.7
  1174.3 54.0 %while.207 = (s32[]{:T(128)}, f32[4,128,256]{2,1,0:T(8,128)}, s32[]{:T(128)}, f32[16,4,128,128]{3,2,1,0:T(8,128)}, f32[16,4,128,256]{3,2,1,0:T(8,128)}, /*index=5*/s32[]{:T(128)}, s32[]{:T(128)}) while((s32[]{:T(128)}, f32[4,128,256]{2,1,0:T(8,128)}, s32[]{:T(128)}, f32[16,4,128,128]{3,2,1,0:T(8,128)}, ...), condition=%wide.region_34.38_spmd.clone, body=%wide.region_33.37_spmd.clone.sunk | while | flops 201850880 | bytes 3410535 | solution.py:34
  1232.8 259.2 %while.205 = (s32[]{:T(128)}, f32[4,128,128]{2,1,0:T(8,128)}, f32[4,128,256]{2,1,0:T(8,128)}, f32[4,4,64,128]{3,2,0,1:T(8,128)}, f32[4,4,64,256]{3,2,1,0:T(8,128...) while((s32[]{:T(128)}, f32[4,128,128]{2,1,0:T(8,128)}, ...), condition=%wide.region_45.49_spmd.clone.clone, body=%wide.region_35.48_spmd.clone.clone.sunk | while | flops 1121261568 | bytes 23002360 | solution.py:148
  1247.2 20.3 custom-call.30
  1311.9 20.3 custom-call.30
  1376.6 20.3 custom-call.30
  1441.3 20.3 custom-call.30
  1517.8 7.3 fusion.322
  1525.2 14.6 reshape.1098
  1542.6 7.3 copy.511
  1549.8 4.6 fusion.324
  1554.4 11.8 reshape.1091
  1575.9 6.2 copy.529
  1584.1 4.9 psum.86
  1590.6 19.4 all-reduce.39.cloned.1.call-done
  1611.5 65.1 %all-reduce.25 = (f32[2,1024]{1,0:T(2,128)}, f32[4,2,512]{2,1,0:T(2,128)}, f32[4,1024]{1,0:T(4,128)}, f32[4]{0:T(128)}, f32[4]{0:T(128)}, /*index=5*/f32[256]{0:T(256)}) all-reduce(f32[2,1024]{1,0:T(2,128)S(1)} %pad_maximum_fusion.7, f32[4,2,512]{2,1,0:T(2,128)S(1)} %reshape.1097, ...), channel_id=1, replica_groups=mesh['dp'=16,'tensor'=2] {'dp'}, use_global_device_ids=true, to_apply=%region_52.56 | all-reduce | flops 10504 | bytes 83520 | tf_op jit(solution)/shard_map/psum | solution.py:402
  1679.9 356.5 %all-reduce.37.cloned.1.call-done = (f32[1024,2,512]{2,1,0:T(2,128)}, f32[1024,2,1024]{2,1,0:T(2,128)}, f32[1024,2,1408]{2,1,0:T(2,128)}) async-done(((f32[1024,2,512]{2,1,0:T(2,128)}, f32[1024,2,1024]{2,1,0:T(2,128)}, f32[1024,2,1408]{2,1,0:T(2,128)}), (f32[1024,2,512]{2,1,0:T(2,128)}, f32[1024,2,1024]{2,1,0:T(2,128)}, f32[1024,2,1408]{2,1,0:T(2,128)})) %all-reduce.37.cloned.1.call-update) | async-done | bytes 24117264
  2042.0 71.5 %reduce-scatter.8.cloned.1.call-done = f32[64,1024]{1,0:T(8,128)} async-done(((f32[1024,1024]{1,0:T(8,128)}), f32[64,1024]{1,0:T(8,128)}) %reduce-scatter.8.cloned.1.call-update) | async-done | bytes 262160 | tf_op jit(solution)/shard_map/reduce_scatter | solution.py:398
  2113.5 84.9 %reduce-scatter.12.cloned.1.call-done = f32[64,1408]{1,0:T(8,128)} async-done(((f32[1024,1408]{1,0:T(8,128)}), f32[64,1408]{1,0:T(8,128)}) %reduce-scatter.12.cloned.1.call-update) | async-done | bytes 360464
  (1144 shorter events, 794.8 us)
Async XLA Ops:
  7.2 29.1 %copy-start.3 = (bf16[256,1024]{1,0:T(8,128)(2,1)S(1)}, bf16[256,1024]{1,0:T(8,128)(2,1)}, u32[]{:S(2)}) copy-start(bf16[256,1024]{1,0:T(8,128)(2,1)} %param.33) | copy-start | bytes 1572868
  7.2 29.0 %copy-start.116 = (bf16[2,1024]{1,0:T(2,128)(2,1)S(1)}, bf16[2,1024]{1,0:T(2,128)(2,1)}, u32[]{:S(2)}) copy-start(bf16[2,1024]{1,0:T(2,128)(2,1)} %param.36) | copy-start | bytes 12292
  7.2 29.4 %copy-start.121 = (f32[4]{0:T(128)S(1)}, f32[4]{0:T(128)}, u32[]{:S(2)}) copy-start(f32[4]{0:T(128)} %param.43) | copy-start | bytes 52
  7.2 30.2 %copy-start.119 = (bf16[4,2,512]{2,1,0:T(2,128)(2,1)S(1)}, bf16[4,2,512]{2,1,0:T(2,128)(2,1)}, u32[]{:S(2)}) copy-start(bf16[4,2,512]{2,1,0:T(2,128)(2,1)} %param.40) | copy-start | bytes 24580
  7.2 30.2 %copy-start.126 = (s32[4]{0:T(128)S(1)}, s32[4]{0:T(128)}, u32[]{:S(2)}) copy-start(s32[4]{0:T(128)} %param.35) | copy-start | bytes 52
  7.2 31.9 %copy-start.120 = (bf16[4,1024]{1,0:T(4,128)(2,1)S(1)}, bf16[4,1024]{1,0:T(4,128)(2,1)}, u32[]{:S(2)}) copy-start(bf16[4,1024]{1,0:T(4,128)(2,1)} %param.41) | copy-start | bytes 24580
  7.3 47.4 %all-gather.14.cloned.1.call-start = ((), (), s32[]{:S(2)}) async-start(), calls=%async_computation.3 | async-start | bytes 2228224 | tf_op jit(solution)/shard_map/all_gather | solution.py:260
  8.0 98.3 %all-gather.16.cloned.1.call-start = ((), (), s32[]{:S(2)}) async-start(), calls=%async_computation.4 | async-start | bytes 4456448 | tf_op jit(solution)/shard_map/all_gather | solution.py:261
  8.7 365.7 %all-gather.24.cloned.1.call-start = ((), (), s32[]{:S(2)}) async-start(), calls=%async_computation.11 | async-start | bytes 4456448 | tf_op jit(solution)/shard_map/all_gather | solution.py:22
  36.3 73.7 %copy-start.88 = (f32[256]{0:T(256)}, f32[256]{0:T(256)S(1)}, u32[]{:S(2)}) copy-start(f32[256]{0:T(256)S(1)} %add_rsqrt_fusion.3) | copy-start | bytes 3076
  36.3 73.7 %copy-start.64 = (f32[1,1024]{1,0:T(1,128)}, f32[1,1024]{1,0:T(1,128)S(1)}, u32[]{:S(2)}) copy-start(f32[1,1024]{1,0:T(1,128)S(1)} %get-tuple-element.5036) | copy-start | bytes 12292
  36.3 814.8 %copy-start.71 = (f32[1,1024]{1,0:T(1,128)}, f32[1,1024]{1,0:T(1,128)S(1)}, u32[]{:S(2)}) copy-start(f32[1,1024]{1,0:T(1,128)S(1)} %get-tuple-element.5035) | copy-start | bytes 12292
  38.5 78.1 %copy-start.107 = (f32[256]{0:T(256)}, f32[256]{0:T(256)S(1)}, u32[]{:S(2)}) copy-start(f32[256]{0:T(256)S(1)} %get-tuple-element.5037) | copy-start | bytes 3076
  38.5 78.1 %copy-start.109 = (f32[256]{0:T(256)}, f32[256]{0:T(256)S(1)}, u32[]{:S(2)}) copy-start(f32[256]{0:T(256)S(1)} %get-tuple-element.5038) | copy-start | bytes 3076
  38.5 78.1 %copy-start.111 = (f32[256]{0:T(256)}, f32[256]{0:T(256)S(1)}, u32[]{:S(2)}) copy-start(f32[256]{0:T(256)S(1)} %get-tuple-element.5039) | copy-start | bytes 3076
  38.5 78.1 %copy-start.113 = (f32[256]{0:T(256)}, f32[256]{0:T(256)S(1)}, u32[]{:S(2)}) copy-start(f32[256]{0:T(256)S(1)} %get-tuple-element.5040) | copy-start | bytes 3076
  39.1 77.5 %copy-start.78 = (f32[1,2048]{1,0:T(1,128)}, f32[1,2048]{1,0:T(1,128)S(1)}, u32[]{:S(2)}) copy-start(f32[1,2048]{1,0:T(1,128)S(1)} %get-tuple-element.5028) | copy-start | bytes 24580
  39.2 77.5 %copy-start.80 = (f32[1,2048]{1,0:T(1,128)}, f32[1,2048]{1,0:T(1,128)S(1)}, u32[]{:S(2)}) copy-start(f32[1,2048]{1,0:T(1,128)S(1)} %get-tuple-element.5029) | copy-start | bytes 24580
  39.2 77.5 %copy-start.82 = (f32[1,2048]{1,0:T(1,128)}, f32[1,2048]{1,0:T(1,128)S(1)}, u32[]{:S(2)}) copy-start(f32[1,2048]{1,0:T(1,128)S(1)} %get-tuple-element.5030) | copy-start | bytes 24580
  39.2 77.5 %copy-start.84 = (f32[1,2048]{1,0:T(1,128)}, f32[1,2048]{1,0:T(1,128)S(1)}, u32[]{:S(2)}) copy-start(f32[1,2048]{1,0:T(1,128)S(1)} %get-tuple-element.5031) | copy-start | bytes 24580
  56.8 53.1 %copy-start.26 = (bf16[128,8,2,512]{3,1,2,0:T(8,128)(2,1)}, bf16[128,8,2,512]{3,1,2,0:T(8,128)(2,1)S(1)}, u32[]{:S(2)}) copy-start(bf16[128,8,2,512]{3,1,2,0:T(8,128)(2,1)S(1)} %copy.585) | copy-start | bytes 6291460
  113.3 3.0 collective-permute-start
  322.1 128.4 %copy-start.48 = (f32[128,128]{1,0:T(8,128)}, f32[128,128]{1,0:T(8,128)S(1)}, u32[]{:S(2)}) copy-start(f32[128,128]{1,0:T(8,128)S(1)} %get-tuple-element.6628) | copy-start | bytes 196612
  322.1 128.4 %copy-start.74 = (f32[4,4,64]{2,1,0:T(4,128)}, f32[4,4,64]{2,1,0:T(4,128)S(1)}, u32[]{:S(2)}) copy-start(f32[4,4,64]{2,1,0:T(4,128)S(1)} %get-tuple-element.6489) | copy-start | bytes 12292
  322.1 128.4 %copy-start.76 = (f32[4,4,64]{2,1,0:T(4,128)}, f32[4,4,64]{2,1,0:T(4,128)S(1)}, u32[]{:S(2)}) copy-start(f32[4,4,64]{2,1,0:T(4,128)S(1)} %get-tuple-element.6484) | copy-start | bytes 12292
  322.1 128.4 %copy-start.90 = (f32[4,4,64,1]{2,1,3,0:T(4,128)}, f32[4,4,64,1]{2,1,3,0:T(4,128)S(1)}, u32[]{:S(2)}) copy-start(f32[4,4,64,1]{2,1,3,0:T(4,128)S(1)} %get-tuple-element.6477) | copy-start | bytes 12292
  322.1 128.4 %copy-start.91 = (f32[4,4,64,1]{2,1,3,0:T(4,128)}, f32[4,4,64,1]{2,1,3,0:T(4,128)S(1)}, u32[]{:S(2)}) copy-start(f32[4,4,64,1]{2,1,3,0:T(4,128)S(1)} %get-tuple-element.6471) | copy-start | bytes 12292
  322.1 128.3 %all-gather.26.cloned.1.call-start = ((), (), s32[]{:S(2)}) async-start(), calls=%async_computation.12 | async-start | bytes 8912896 | tf_op jit(solution)/shard_map/all_gather | solution.py:22
  322.7 389.4 %all-gather.18.cloned.1.call-start = ((), (), s32[]{:S(2)}) async-start(), calls=%async_computation.5 | async-start | bytes 2228224 | tf_op jit(solution)/shard_map/all_gather | solution.py:263
  323.3 393.2 %all-gather.20.cloned.1.call-start = ((), (), s32[]{:S(2)}) async-start(), calls=%async_computation.7 | async-start | bytes 6127616 | tf_op jit(solution)/shard_map/all_gather | solution.py:320
  323.9 430.3 %all-reduce.33.cloned.1.call-start = ((), (), s32[]{:S(2)}) async-start(), calls=%async_computation.6 | async-start | bytes 2097152 | tf_op jit(solution)/shard_map/psum | solution.py:314
  325.0 125.5 %copy-start.117 = (f32[256]{0:T(256)}, f32[256]{0:T(256)S(1)}, u32[]{:S(2)}) copy-start(f32[256]{0:T(256)S(1)} %convert_element_type.144) | copy-start | bytes 3076
  715.7 85.4 %all-gather.22.cloned.1.call-start = ((), (), s32[]{:S(2)}) async-start(), calls=%async_computation.8 | async-start | bytes 3063808 | tf_op jit(solution)/shard_map/all_gather | solution.py:321
  716.4 132.0 %all-reduce.35.cloned.1.call-start = ((), (), s32[]{:S(2)}) async-start(), calls=%async_computation.9 | async-start | bytes 2097152 | tf_op jit(solution)/shard_map/psum | solution.py:342
  716.5 37.6 %copy-start.4 = (bf16[256,1024]{1,0:T(8,128)(2,1)S(1)}, bf16[256,1024]{1,0:T(8,128)(2,1)}, u32[]{:S(2)}) copy-start(bf16[256,1024]{1,0:T(8,128)(2,1)} %param.33) | copy-start | bytes 1572868
  755.6 95.5 %copy-start.100 = (f32[256]{0:T(256)}, f32[256]{0:T(256)S(1)}, u32[]{:S(2)}) copy-start(f32[256]{0:T(256)S(1)} %add_rsqrt_fusion.2) | copy-start | bytes 3076
  756.6 44.5 %copy-start.57 = (bf16[256,1024]{1,0:T(8,128)(2,1)S(1)}, bf16[256,1024]{1,0:T(8,128)(2,1)}, u32[]{:S(2)}) copy-start(bf16[256,1024]{1,0:T(8,128)(2,1)} %param.34) | copy-start | bytes 1572868
  809.9 286.4 %all-gather.28.cloned.1.call-start = ((), (), s32[]{:S(2)}) async-start(), calls=%async_computation.13 | async-start | bytes 4456448 | tf_op jit(solution)/shard_map/all_gather | solution.py:22
  811.8 354.8 %all-gather.30.cloned.1.call-start = ((), (), s32[]{:S(2)}) async-start(), calls=%async_computation.14 | async-start | bytes 8912896 | tf_op jit(solution)/shard_map/all_gather | solution.py:22
  871.9 220.7 %copy-start.49 = (f32[128,128]{1,0:T(8,128)S(1)}, f32[128,128]{1,0:T(8,128)}, u32[]{:S(2)}) copy-start(f32[128,128]{1,0:T(8,128)} %copy-done.48) | copy-start | bytes 196612
  1091.6 497.6 %reduce-scatter.10.cloned.1.call-start = ((), (), s32[]{:S(2)}) async-start(), calls=%async_computation.15 | async-start | bytes 557056
  1507.5 4.0 collective-permute-start.1
  1511.4 98.5 %all-reduce.39.cloned.1.call-start = ((), (), s32[]{:S(2)}) async-start(), calls=%async_computation.18 | async-start | bytes 2097152 | tf_op jit(solution)/shard_map/psum | solution.py:329
  1517.8 518.7 %all-reduce.37.cloned.1.call-start = ((), (), s32[]{:S(2)}) async-start(), calls=%async_computation.17 | async-start | bytes 48234496
  1566.2 547.3 %reduce-scatter.8.cloned.1.call-start = ((), (), s32[]{:S(2)}) async-start(), calls=%async_computation.10 | async-start | bytes 4456448 | tf_op jit(solution)/shard_map/reduce_scatter | solution.py:398
  1570.4 628.0 %reduce-scatter.12.cloned.1.call-start = ((), (), s32[]{:S(2)}) async-start(), calls=%async_computation.16 | async-start | bytes 6127616
  1582.2 29.3 %copy-start.115 = (f32[1024]{0:T(1024)S(1)}, f32[1024]{0:T(1024)}, u32[]{:S(2)}) copy-start(f32[1024]{0:T(1024)} %get-tuple-element.4619) | copy-start | bytes 12292
  1609.9 68.7 %copy-start.60 = (bf16[256,1024]{1,0:T(8,128)(2,1)S(1)}, bf16[256,1024]{1,0:T(8,128)(2,1)}, u32[]{:S(2)}) copy-start(bf16[256,1024]{1,0:T(8,128)(2,1)} %get-tuple-element.4925) | copy-start | bytes 1572868
  (142 other events, 678.8 us)
Sparse Core Ops, SparseCore 0:
  10.3 44.3 all-gather.13
  56.8 49.4 all-gather.15
  322.3 52.1 all-gather.23
  377.1 73.3 all-gather.25
  452.5 39.6 all-gather.17
  494.3 57.9 all-gather.19
  715.8 38.3 all-reduce.32
  756.7 44.3 all-gather.21
  810.0 38.3 all-reduce.34
  851.0 50.9 all-gather.27
  1091.7 74.8 all-gather.29
  1511.5 55.9 reduce-scatter.9
  1570.6 39.3 all-reduce.38
  1614.7 421.7 all-reduce.36
  2041.2 72.2 reduce-scatter.7
  2117.8 80.5 reduce-scatter.11
where the time goes:
time: 2220 us; the launch traced here: 2210 us
  waiting for transfers between devices  889 us (40%)
  other arithmetic  474 us (21%)
  matrix products  379 us (17%)
  local copies, waits for them, and re-layouts  344 us (15%)
  blocking collectives  94.9 us (4%)
    unnamed x19, waiting for transfers between devices  445 us
    another operation x48, other arithmetic, group_parts(): lax.linalg.triangular_solve(system, right, left_side=True, lower=True)  345 us
    all_gather x4, waiting for transfers between devices, carried_in(): pieces = jax.tree.map(lambda part: lax.all_gather(part, axis), value)  182 us
    dot_general x30, matrix products, compose(): jnp.einsum('hij,hjv->hiv', later[0], earlier[1], precision=high_accuracy_...  76.5 us
    reduce_scatter x1, waiting for transfers between devices, local(): lax.psum_scatter(grad_out_weight, 'dp', scatter_dimension=0, tiled=True)  71.5 us
    psum x1, blocking collectives, local(): lax.psum((jnp.stack([gain_one_grad, gain_two_grad]), grad_taps[:, :2 * wi...  65.1 us
    dynamic_slice x40, local copies, waits for them, and re-layouts, local_outputs(): lax.scan(advance, state_sequence, (query_rows_local, key_rows, value_rows...  55.7 us
    unnamed x257, local copies, waits for them, and re-layouts  55.5 us
  transfers between devices with their start and end apart: 18, of which 13 were waited for; matrix products, arithmetic and copies ran while one was open for 28% of the time, Pallas kernels for 0%

commit v1 on v0

v1 whole, which is shorter than its diff:
```python
import jax
import jax.numpy as jnp
from jax import lax
from jax.sharding import PartitionSpec as P

DK = 128
DV = 256
GROUP = 64


LONGEST_BLOCKS = 32

accuracy = lax.Precision.HIGH


def shifted(block, axis, distance):
    devices = range(lax.axis_size(axis))
    route = [(i - distance, i) for i in devices if i - distance in devices]
    return lax.ppermute(block, axis, route)


def round_low(values):
    return lax.optimization_barrier(values.astype(jnp.bfloat16)).astype(jnp.float32)


def unit_rows(values, epsilon):
    return values * lax.rsqrt(jnp.mean(values * values, axis=-1, keepdims=True) + epsilon)


def unit_sphere(values):
    return values * lax.rsqrt(jnp.sum(values * values, axis=-1, keepdims=True) + 1e-06)


def norm_back(grad_unit, unit_value, scale_rows):
    return scale_rows * (
        grad_unit - unit_value * jnp.mean(grad_unit * unit_value, axis=-1, keepdims=True)
    )


def to_blocks(rows_data, size):
    count = rows_data.shape[0] // size
    return rows_data.reshape(count, size, rows_data.shape[1], -1).transpose(0, 2, 1, 3)


def from_blocks(blocked):
    return blocked.transpose(0, 2, 1, 3).reshape(-1, blocked.shape[1], blocked.shape[3])


def matmul(left, right):
    return jnp.einsum("...ij,...jk->...ik", left, right, precision=accuracy)


def matmul_tn(left, right):
    return jnp.einsum("...ji,...jk->...ik", left, right, precision=accuracy)


def matmul_nt(left, right):
    return jnp.einsum("...ij,...kj->...ik", left, right, precision=accuracy)


def pair_sum(part, axis):
    if lax.axis_size(axis) != 2:
        return lax.psum(part, axis).astype(jnp.float32)
    other = lax.ppermute(part, axis, [(0, 1), (1, 0)])
    return part.astype(jnp.float32) + other.astype(jnp.float32)


def carried(mat, vec, axis, direction, window):
    size = mat.shape[-1]
    packed = jnp.concatenate([mat, vec], axis=-1).astype(jnp.bfloat16)
    window = min(window, lax.axis_size(axis) - 1)
    total = shifted(packed, axis, direction).astype(jnp.float32)
    reach = 1
    while reach < window:
        low = total.astype(jnp.bfloat16)
        last = 2 * reach >= window
        if last:
            low = low[..., size:]
        far = shifted(low, axis, direction * reach).astype(jnp.float32)
        product = matmul(total[..., :size], far)
        if last:
            return product + total[..., size:]
        total = product + jnp.concatenate(
            [jnp.zeros_like(total[..., :size]), total[..., size:]], axis=-1
        )
        reach = 2 * reach
    return total[..., size:]


def inverse_of(system):
    length = system.shape[-1]
    row = lax.broadcasted_iota(jnp.int32, (length, length), 0)
    col = lax.broadcasted_iota(jnp.int32, (length, length), 1)
    inverse = None
    half = 1
    while half < length:
        mask = (row // (2 * half) == col // (2 * half)) & (row // half > col // half)
        corner = jnp.where(mask, system, 0.0)
        if inverse is None:
            inverse = jnp.eye(length, dtype=jnp.float32) - corner
        else:
            inverse = inverse - matmul(matmul(inverse, corner), inverse)
        half = 2 * half
    return inverse


@jax.custom_vjp
def solve(system, right):
    return matmul(inverse_of(system), right)


def solve_keep(system, right):
    inverse = inverse_of(system)
    solved = matmul(inverse, right)
    return solved, (inverse, solved)


def solve_back(kept, grad):
    inverse, solved = kept
    grad_right = matmul_tn(inverse, grad)
    return -matmul_nt(grad_right, solved), grad_right


solve.defvjp(solve_keep, solve_back)


def block_parts(queries, keys, values, betas, log_decay):
    length = keys.shape[-2]
    key_size = keys.shape[-1]
    row = lax.broadcasted_iota(jnp.int32, (length, length), 0)
    col = lax.broadcasted_iota(jnp.int32, (length, length), 1)
    running = jnp.einsum(
        "...c,cd->...d",
        log_decay,
        (row <= col).astype(jnp.float32),
        precision=lax.Precision.HIGHEST,
    )
    spread = running[..., :, None] - running[..., None, :]
    ratio = jnp.where(row >= col, jnp.exp(jnp.minimum(spread, 0.0)), 0.0)
    strict = jnp.where(row > col, ratio, 0.0)
    products = matmul_nt(jnp.concatenate([keys, queries], axis=-2), keys)
    inner, across = products[..., :length, :], products[..., length:, :]
    system = jnp.eye(length, dtype=jnp.float32) + betas[..., None] * strict * inner
    decay = jnp.exp(running)
    right = jnp.concatenate(
        [(betas * decay)[..., None] * keys, betas[..., None] * values], axis=-1
    )
    solved = solve(system, right)
    trailing = jnp.exp(running[..., -1:] - running)[..., None] * keys
    written = matmul_tn(trailing, solved)
    step_a = (
        jnp.exp(running[..., -1])[..., None, None] * jnp.eye(key_size, dtype=jnp.float32)
        - written[..., :key_size]
    )
    scale = key_size ** (-0.5)
    return (
        step_a,
        written[..., key_size:],
        solved[..., :key_size],
        solved[..., key_size:],
        scale * across * ratio,
        scale * decay[..., None] * queries,
    )


def front(extended, proj_ab, conv_taps, decay_log, decay_bias, inside):
    row_count = proj_ab.shape[0]
    head_count = decay_log.shape[0]
    taps = conv_taps.shape[0]
    conv_sum = conv_taps[0] * extended[0:row_count] * inside[0]
    for tap_index in range(1, taps):
        conv_sum = (
            conv_sum
            + conv_taps[tap_index] * extended[tap_index : tap_index + row_count] * inside[tap_index]
        )
    activated = jax.nn.silu(conv_sum)
    width_k = head_count * DK
    query_rows_local = unit_sphere(activated[:, :width_k].reshape(row_count, head_count, DK))
    key_rows = unit_sphere(activated[:, width_k : 2 * width_k].reshape(row_count, head_count, DK))
    value_rows = activated[:, 2 * width_k :].reshape(row_count, head_count, DV)
    beta_rows = jax.nn.sigmoid(proj_ab[:, head_count:])
    log_decay = -jnp.exp(decay_log) * jax.nn.softplus(proj_ab[:, :head_count] + decay_bias)
    return (query_rows_local, key_rows, value_rows, beta_rows, log_decay)


def gated_output(heads_out, gate_raw, output_gain):
    gate_heads = gate_raw.reshape(heads_out.shape)
    return (unit_rows(heads_out, 1e-05) * output_gain * jax.nn.silu(gate_heads)).reshape(
        gate_raw.shape
    )


def contract_rows(left, right):
    return lax.dot_general(
        left, right, (((0,), (0,)), ((), ())), preferred_element_type=jnp.float32
    )


def contract_cols(left, right):
    return lax.dot_general(
        left, right, (((1,), (1,)), ((), ())), preferred_element_type=jnp.float32
    )


def summed_rows(left, right):
    part = contract_rows(left, right).astype(jnp.bfloat16)
    share = lax.psum_scatter(part, "dp", scatter_dimension=0, tiled=True)
    return share.astype(jnp.float32)


def local(
    tokens,
    cotangent,
    lengths,
    norm_gains,
    query_key_weight,
    value_gate_weight,
    decay_beta_weight,
    conv_query_key,
    conv_value,
    decay_log,
    decay_bias,
    output_gain,
    out_weight,
    gate_up_weight,
    down_weight,
):
    row_count, width = tokens.shape
    head_count = decay_log.shape[0]
    width_k = head_count * DK
    width_v = head_count * DV
    taps = conv_query_key.shape[0]
    rim_rows = taps - 1
    first_row = lax.axis_index("dp") * row_count
    positions = first_row + lax.broadcasted_iota(jnp.int32, (row_count,), 0)
    seq_starts = (jnp.cumsum(lengths) - lengths) * GROUP
    seg_first = jnp.max(
        jnp.where(seq_starts[None, :] <= positions[:, None], seq_starts[None, :], 0), axis=1
    )
    block_first = positions[::GROUP]
    keep_flags = 1.0 - jnp.any(seq_starts[None, :] == block_first[:, None], axis=1).astype(
        jnp.float32
    )
    inside = jnp.stack(
        [
            (positions - (rim_rows - tap_index) >= seg_first).astype(jnp.float32)[:, None]
            for tap_index in range(taps)
        ]
    )
    gains = norm_gains.astype(jnp.float32)
    inputs = tokens.astype(jnp.float32)
    scale_one = lax.rsqrt(jnp.mean(inputs * inputs, axis=-1, keepdims=True) + 1e-06)
    unit_one = inputs * scale_one
    normed = (unit_one * gains[0]).astype(jnp.bfloat16)
    full_in = lax.all_gather(
        jnp.concatenate(
            [
                query_key_weight.reshape(-1, 2 * width_k),
                value_gate_weight.reshape(-1, 2 * width_v),
                decay_beta_weight.reshape(-1, 2 * head_count),
            ],
            axis=1,
        ),
        "dp",
        axis=0,
        tiled=True,
    )
    full_out = lax.all_gather(out_weight, "dp", axis=0, tiled=True)
    width_c = 2 * width_k + width_v
    width_g = width_c + width_v
    projected = jnp.dot(normed, full_in, preferred_element_type=jnp.float32)
    pre_conv = projected[:, :width_c].astype(jnp.bfloat16)
    gate_raw = projected[:, width_c:width_g]
    proj_ab = projected[:, width_g:]
    rim = shifted(pre_conv[row_count - rim_rows :], "dp", 1)
    extended = jnp.concatenate([rim, pre_conv], axis=0).astype(jnp.float32)
    conv_taps = jnp.concatenate(
        [conv_query_key.reshape(taps, 2 * width_k), conv_value], axis=1
    ).astype(jnp.float32)

    def front_piece(ext_rows, ab_rows, tap_rows, log_rate, rate_bias):
        return front(ext_rows, ab_rows, tap_rows, log_rate, rate_bias, inside)

    fronted, front_back = jax.vjp(front_piece, extended, proj_ab, conv_taps, decay_log, decay_bias)
    query_rows_local, key_rows, value_rows, beta_rows, log_decay = fronted
    block_q = to_blocks(round_low(query_rows_local), GROUP)
    block_k = to_blocks(round_low(key_rows), GROUP)
    block_v = to_blocks(round_low(value_rows), GROUP)
    block_b = to_blocks(beta_rows[:, :, None], GROUP)[..., 0]
    block_g = to_blocks(log_decay[:, :, None], GROUP)[..., 0]

    parts, parts_back = jax.vjp(block_parts, block_q, block_k, block_v, block_b, block_g)
    step_a, step_b, erase, write, scores, reads = parts
    keep = keep_flags[:, None, None, None]
    block_count = step_a.shape[0]
    window = -(-(LONGEST_BLOCKS - 1) // block_count)
    kept_a = keep * step_a
    maps = [jnp.concatenate([kept_a[0], step_b[0]], axis=-1)]
    no_map = jnp.zeros_like(kept_a[0])
    for j in range(1, block_count):
        maps.append(
            matmul(kept_a[j], maps[-1]) + jnp.concatenate([no_map, step_b[j]], axis=-1)
        )
    entering = carried(maps[-1][..., :DK], maps[-1][..., DK:], "dp", 1, window)
    states = entering[None]
    if block_count > 1:
        before = jnp.stack(maps[:-1])
        states = jnp.concatenate(
            [states, matmul(before[..., :DK], entering[None]) + before[..., DK:]], axis=0
        )
    seen = keep * states
    recalled = matmul(jnp.concatenate([erase, reads], axis=-2), seen)
    fresh = write - recalled[..., :GROUP, :]
    block_out = recalled[..., GROUP:, :] + matmul(scores, fresh)
    heads_out = from_blocks(block_out)
    gated, gated_back = jax.vjp(gated_output, heads_out, gate_raw, output_gain.astype(jnp.float32))
    gated_low = gated.astype(jnp.bfloat16)
    mixed_sum = pair_sum(contract_cols(gated_low, full_out).astype(jnp.bfloat16), "tensor")
    residual = inputs + mixed_sum
    scale_two = lax.rsqrt(jnp.mean(residual * residual, axis=-1, keepdims=True) + 1e-06)
    unit_two = residual * scale_two
    normed_two = (unit_two * gains[1]).astype(jnp.bfloat16)
    ff_local = down_weight.shape[1]
    matrix_gu = lax.all_gather(
        gate_up_weight.reshape(-1, 2 * ff_local), "dp", axis=0, tiled=True
    )
    full_down = lax.all_gather(down_weight, "dp", axis=0, tiled=True)
    up_gate = jnp.dot(normed_two, matrix_gu, preferred_element_type=jnp.float32)
    gate_two = up_gate[:, :ff_local]
    up_two = up_gate[:, ff_local:]
    hidden = (jax.nn.silu(gate_two) * up_two).astype(jnp.bfloat16)
    mlp_total = pair_sum(contract_cols(hidden, full_down).astype(jnp.bfloat16), "tensor")
    output = (residual + mlp_total).astype(jnp.bfloat16)
    grad_out = cotangent.astype(jnp.float32)
    grad_hidden = jnp.dot(cotangent, full_down, preferred_element_type=jnp.float32)
    share_down = summed_rows(cotangent, hidden)
    sigma_two = jax.nn.sigmoid(gate_two)
    grad_gate_two = grad_hidden * up_two * sigma_two * (1.0 + gate_two * (1.0 - sigma_two))
    grad_up_two = grad_hidden * gate_two * sigma_two
    grad_gu_low = jnp.concatenate([grad_gate_two, grad_up_two], axis=1).astype(jnp.bfloat16)
    share_gu = summed_rows(normed_two, grad_gu_low)
    grad_normed_two_part = contract_cols(grad_gu_low, matrix_gu)
    grad_normed_two = pair_sum(grad_normed_two_part.astype(jnp.bfloat16), "tensor")
    gain_two_grad = jnp.sum(grad_normed_two * unit_two, axis=0)
    grad_residual = grad_out + norm_back(grad_normed_two * gains[1], unit_two, scale_two)
    grad_res_low = grad_residual.astype(jnp.bfloat16)
    grad_gated = jnp.dot(grad_res_low, full_out, preferred_element_type=jnp.float32)
    share_out = summed_rows(grad_res_low, gated_low)
    grad_heads, grad_gate_raw, grad_gain_part = gated_back(grad_gated)
    grad_blocks = to_blocks(grad_heads, GROUP)
    grad_fresh = matmul_tn(scores, grad_blocks)
    both = jnp.concatenate([-grad_fresh, grad_blocks], axis=-2)
    grad_seen = keep * matmul_tn(jnp.concatenate([erase, reads], axis=-2), both)
    flipped = jnp.swapaxes(kept_a, -1, -2)
    maps_back = [jnp.concatenate([flipped[-1], grad_seen[-1]], axis=-1)]
    for j in range(block_count - 2, -1, -1):
        maps_back.append(
            matmul(flipped[j], maps_back[-1]) + jnp.concatenate([no_map, grad_seen[j]], axis=-1)
        )
    leaving = carried(maps_back[-1][..., :DK], maps_back[-1][..., DK:], "dp", -1, window)
    grad_states = leaving[None]
    if block_count > 1:
        after = jnp.stack(maps_back[-2::-1])
        grad_states = jnp.concatenate(
            [matmul(after[..., :DK], leaving[None]) + after[..., DK:], grad_states], axis=0
        )
    grad_factors = matmul_nt(both, seen)
    grad_bq, grad_bk, grad_bv, grad_bb, grad_bg = parts_back(
        (
            matmul_nt(grad_states, seen),
            grad_states,
            grad_factors[..., :GROUP, :],
            grad_fresh,
            matmul_nt(grad_blocks, fresh),
            grad_factors[..., GROUP:, :],
        )
    )
    grad_queries = from_blocks(grad_bq)
    grad_keys = from_blocks(grad_bk)
    grad_values = from_blocks(grad_bv)
    grad_betas = from_blocks(grad_bb[..., None])[..., 0]
    grad_decays = from_blocks(grad_bg[..., None])[..., 0]
    grad_ext, grad_ab, grad_taps, grad_decay_log, grad_decay_bias = front_back(
        (grad_queries, grad_keys, grad_values, grad_betas, grad_decays)
    )
    rim_grad = shifted(grad_ext[:rim_rows], "dp", -1)
    grad_pre = grad_ext[rim_rows:] + jnp.concatenate(
        [jnp.zeros((row_count - rim_rows, grad_ext.shape[1]), jnp.float32), rim_grad], axis=0
    )
    grad_pre_low = grad_pre.astype(jnp.bfloat16)
    grad_in_low = jnp.concatenate(
        [grad_pre_low, grad_gate_raw.astype(jnp.bfloat16), grad_ab.astype(jnp.bfloat16)], axis=1
    )
    share_in = summed_rows(normed, grad_in_low)
    grad_normed = pair_sum(contract_cols(grad_in_low, full_in).astype(jnp.bfloat16), "tensor")
    grad_gain_out = pair_sum(grad_gain_part, "tensor")
    gain_one_grad = jnp.sum(grad_normed * unit_one, axis=0)
    grad_tokens = grad_residual + norm_back(grad_normed * gains[0], unit_one, scale_one)
    small_parts = (
        gain_one_grad,
        gain_two_grad,
        grad_taps[:, : 2 * width_k].reshape(-1),
        grad_taps[:, 2 * width_k :].reshape(-1),
        grad_gain_out,
        grad_decay_log,
        grad_decay_bias,
    )
    small = lax.psum(jnp.concatenate(small_parts), "dp")
    sums = []
    at = 0
    for part in small_parts:
        sums.append(small[at : at + part.shape[0]])
        at += part.shape[0]
    return (
        output,
        grad_tokens,
        jnp.stack(sums[:2]),
        share_in[:, : 2 * width_k].reshape(query_key_weight.shape),
        share_in[:, 2 * width_k : width_g].reshape(value_gate_weight.shape),
        share_in[:, width_g:].reshape(decay_beta_weight.shape),
        sums[2].reshape(conv_query_key.shape),
        sums[3].reshape(conv_value.shape),
        sums[5],
        sums[6],
        sums[4],
        share_out,
        share_gu.reshape(gate_up_weight.shape),
        share_down,
    )


def solution(mesh):
    in_specs = (
        P("dp", None),
        P("dp", None),
        P(),
        P(),
        P("dp", None, "tensor"),
        P("dp", None, "tensor"),
        P("dp", None, "tensor"),
        P(None, None, "tensor"),
        P(None, "tensor"),
        P("tensor"),
        P("tensor"),
        P(),
        P("dp", "tensor"),
        P("dp", None, "tensor"),
        P("dp", "tensor"),
    )
    out_specs = (
        P("dp", None),
        P("dp", None),
        P(),
        P("dp", None, "tensor"),
        P("dp", None, "tensor"),
        P("dp", None, "tensor"),
        P(None, None, "tensor"),
        P(None, "tensor"),
        P("tensor"),
        P("tensor"),
        P(),
        P("dp", "tensor"),
        P("dp", None, "tensor"),
        P("dp", "tensor"),
    )
    return jax.shard_map(local, mesh=mesh, in_specs=in_specs, out_specs=out_specs, check_vma=False)
```

time: 2220 us -> 609 us (0.27)
  waiting for transfers between devices: 889 us -> 190 us
  other arithmetic: 474 us -> 73.2 us
  matrix products: 379 us -> 91.5 us
  local copies, waits for them, and re-layouts: 344 us -> 109 us
  starting transfers between devices: 5.08 us -> 63.5 us
  blocking collectives: 94.9 us -> 58.4 us
    unnamed x19 -> x9, waiting for transfers between devices: 445 us -> 1.32 us
    another operation x77 -> x4, other arithmetic: 357 us -> 0.89 us  [the longest x1 0.61 us: local(): jnp.stack(sums[:2])]
    dot_general x174 -> x43, matrix products: 290 us -> 53.4 us  [the longest x27 24.7 us: matmul(): return jnp.einsum('...ij,...jk->...ik', left, right, precision=accuracy)]
    all_gather x9 -> x4, waiting for transfers between devices: 285 us -> 59.7 us  [the longest x1 59.7 us: local(): lax.all_gather(jnp.concatenate([query_key_weight.reshape(-1, 2 * width_k)...]
    psum x3 -> x0, waiting for transfers between devices: 87.2 us -> none  [the longest x1 36.4 us: local(): grad_normed_two = lax.psum(grad_normed_two_part, 'tensor')]
    dynamic_slice x56 -> x0, local copies, waits for them, and re-layouts: 75.4 us -> none  [the longest x40 55.7 us: local_outputs(): lax.scan(advance, state_sequence, (query_rows_local, key_rows, value_rows...]
    ppermute x2 -> x10, starting transfers between devices: 3.65 us -> 57.2 us  [shifted(): return lax.ppermute(block, axis, route)]
    ppermute x0 -> x5, waiting for transfers between devices: none -> 49.1 us  [pair_sum(): other = lax.ppermute(part, axis, [(0, 1), (1, 0)])]
  transfers between devices with their start and end apart: 18 -> 23, of which waited for: 13 -> 15; matrix products, arithmetic and copies ran while one was open for 28% -> 40% of each run, Pallas kernels for 0% -> 0%
where the time goes in v1:
time: 609 us; the launch traced here: 601 us
  waiting for transfers between devices  190 us (31%)
  local copies, waits for them, and re-layouts  109 us (18%)
  matrix products  91.5 us (15%)
  other arithmetic  73.2 us (12%)
  starting transfers between devices  63.5 us (10%)
  blocking collectives  58.4 us (10%)
  between operations  16.9 us (3%)
    all_gather x1, waiting for transfers between devices, local(): lax.all_gather(jnp.concatenate([query_key_weight.reshape(-1, 2 * width_k)...  59.7 us
    psum x1, blocking collectives, local(): small = lax.psum(jnp.concatenate(small_parts), 'dp')  58.4 us
    ppermute x10, starting transfers between devices, shifted(): return lax.ppermute(block, axis, route)  57.2 us
    ppermute x5, waiting for transfers between devices, pair_sum(): other = lax.ppermute(part, axis, [(0, 1), (1, 0)])  49.1 us
    reduce_scatter x3, waiting for transfers between devices, summed_rows(): share = lax.psum_scatter(part, 'dp', scatter_dimension=0, tiled=True)  40.7 us
    ppermute x10, waiting for transfers between devices, shifted(): return lax.ppermute(block, axis, route)  38.7 us
    unnamed x345, local copies, waits for them, and re-layouts  27.6 us
    dot_general x27, matrix products, matmul(): return jnp.einsum('...ij,...jk->...ik', left, right, precision=accuracy)  24.7 us
  transfers between devices with their start and end apart: 23, of which 15 were waited for; matrix products, arithmetic and copies ran while one was open for 40% of the time, Pallas kernels for 0%

profile of v1, /device:TPU:0, one launch (start us, length us, event | category | flops | bytes accessed | tf_op | source)
XLA Modules:
  0.0 601.4 jit_solution(2768147173811580459)
XLA Ops:
  17.5 59.7 %all-gather.5.cloned.1.call-done = bf16[1024,3080]{1,0:T(8,128)(2,1)} async-done(((bf16[64,3080]{1,0:T(8,128)(2,1)}), bf16[1024,3080]{1,0:T(8,128)(2,1)}) %all-gather.5.cloned.1.call-update) | async-done | bytes 6307856 | tf_op jit(solution)/shard_map/all_gather | solution.py:255
  77.1 5.7 fusion.228
  83.1 3.0 collective-permute-start
  93.2 4.2 fusion.6
  128.7 2.6 copy.555
  140.0 3.9 collective-permute-start.1
  145.2 9.5 %collective-permute-start.2 = (bf16[4,128,384]{2,1,0:T(8,128)(2,1)S(1)}, bf16[4,128,384]{2,1,0:T(8,128)(2,1)S(1)}, u32[]{:S(2)}, u32[]{:S(2)}) collective-permute-start(bf16[4,128,384]{2,1,0:T(8,128)(2,1)S(1)} %collective-permute-done.1), channel_id=1, source_target_pairs={{0,2},{2,4},{4,6},{6,8},{8,10},{10,12},{12,14},{14,16},{16,18},{18... | collective-permute-start | bytes 1179656 | tf_op jit(solution)/shard_map/ppermute | solution.py:19
  157.3 19.3 %collective-permute-start.3 = (bf16[4,128,384]{2,1,0:T(8,128)(2,1)}, bf16[4,128,384]{2,1,0:T(8,128)(2,1)}, u32[]{:S(2)}, u32[]{:S(2)}) collective-permute-start(bf16[4,128,384]{2,1,0:T(8,128)(2,1)} %get-tuple-element.200), channel_id=1, source_target_pairs={{0,4},{2,6},{4,8},{6,10},{8,12},{10,14},{12,16},{14,18},{16,20},{1... | collective-permute-start | bytes 1179656 | tf_op jit(solution)/shard_map/ppermute | solution.py:19
  182.9 14.5 %collective-permute-start.4 = (bf16[4,128,256]{2,1,0:T(8,128)(2,1)S(1)}, bf16[4,128,256]{2,1,0:T(8,128)(2,1)S(1)}, u32[]{:S(2)}, u32[]{:S(2)}) collective-permute-start(bf16[4,128,256]{2,1,0:T(8,128)(2,1)S(1)} %slice.544), channel_id=1, source_target_pairs={{0,8},{2,10},{4,12},{6,14},{8,16},{10,18},{12,20},{14,22},{16,24},... | collective-permute-start | bytes 786440 | tf_op jit(solution)/shard_map/ppermute | solution.py:19
  197.9 9.6 %collective-permute-done.4 = bf16[4,128,256]{2,1,0:T(8,128)(2,1)S(1)} collective-permute-done((bf16[4,128,256]{2,1,0:T(8,128)(2,1)S(1)}, bf16[4,128,256]{2,1,0:T(8,128)(2,1)S(1)}, u32[]{:S(2)}, u32[]{:S(2)}) %collective-permute-start.4) | collective-permute-done | bytes 262176 | tf_op jit(solution)/shard_map/ppermute | solution.py:19
  210.1 2.6 multiply_reduce_fusion.10
  212.7 2.9 copy.542
  215.6 3.2 reshape.409
  221.5 2.8 multiply_convert_fusion.4
  224.3 2.6 convolution_convert_fusion.6
  228.2 13.0 %collective-permute-done.5 = bf16[256,1024]{1,0:T(8,128)(2,1)S(1)} collective-permute-done((bf16[256,1024]{1,0:T(8,128)(2,1)S(1)}, bf16[256,1024]{1,0:T(8,128)(2,1)S(1)}, u32[]{:S(2)}, u32[]{:S(2)}) %collective-permute-start.5) | collective-permute-done | bytes 524320 | tf_op jit(solution)/shard_map/ppermute | solution.py:64
  243.1 6.2 %fusion.211 = f32[256,2816]{1,0:T(8,128)} fusion(bf16[1024,2816]{1,0:T(8,128)(2,1)} %all-gather.9.cloned.1.call-done, f32[256,1024]{1,0:T(8,128)} %get-tuple-element.132, f32[1024]{0:T(1024)S(1)} %bitcast.318, f32[256]{0:T(256)} %add_rsqrt_fusion.2), kind=kOutput, calls=%fused_computation.427 | convolution fusion | flops 1477181440 | bytes 9704448 | tf_op jit(solution)/shard_map/dot_general | solution.py:328
  249.3 4.3 multiply_convert_fusion.1
  258.9 11.5 %collective-permute-done.7 = bf16[256,1024]{1,0:T(8,128)(2,1)S(1)} collective-permute-done((bf16[256,1024]{1,0:T(8,128)(2,1)S(1)}, bf16[256,1024]{1,0:T(8,128)(2,1)S(1)}, u32[]{:S(2)}, u32[]{:S(2)}) %collective-permute-start.7) | collective-permute-done | bytes 524320 | tf_op jit(solution)/shard_map/ppermute | solution.py:64
  271.4 9.0 %collective-permute-done.6 = bf16[256,1024]{1,0:T(8,128)(2,1)S(1)} collective-permute-done((bf16[256,1024]{1,0:T(8,128)(2,1)S(1)}, bf16[256,1024]{1,0:T(8,128)(2,1)S(1)}, u32[]{:S(2)}, u32[]{:S(2)}) %collective-permute-start.6) | collective-permute-done | bytes 524320 | tf_op jit(solution)/shard_map/ppermute | solution.py:64
  288.3 2.6 fusion
  290.9 4.6 copy.547
  295.7 3.7 fusion.113
  299.4 2.6 copy.493
  302.0 2.7 reshape.382
  304.7 3.4 fusion.42
  308.1 3.1 reshape.415
  311.2 2.9 copy.474
  314.1 3.3 multiply_reduce_fusion.4
  331.6 4.0 collective-permute-done.9
  338.2 4.3 convolution_convert_fusion.1
  343.8 6.7 %collective-permute-done.10 = bf16[4,128,384]{2,1,0:T(8,128)(2,1)} collective-permute-done((bf16[4,128,384]{2,1,0:T(8,128)(2,1)}, bf16[4,128,384]{2,1,0:T(8,128)(2,1)}, u32[]{:S(2)}, u32[]{:S(2)}) %collective-permute-start.10) | collective-permute-done | bytes 393248 | tf_op jit(solution)/shard_map/ppermute | solution.py:19
  356.3 12.1 %collective-permute-done.11 = bf16[4,128,256]{2,1,0:T(8,128)(2,1)S(1)} collective-permute-done((bf16[4,128,256]{2,1,0:T(8,128)(2,1)S(1)}, bf16[4,128,256]{2,1,0:T(8,128)(2,1)S(1)}, u32[]{:S(2)}, u32[]{:S(2)}) %collective-permute-start.11) | collective-permute-done | bytes 262176 | tf_op jit(solution)/shard_map/ppermute | solution.py:19
  381.2 3.0 multiply_reduce_fusion.13
  393.5 2.8 copy.546
  408.3 2.8 multiply_bitcast_fusion
  412.9 2.6 reshape.411
  415.5 2.6 reshape.412
  418.2 2.7 copy.544
  420.9 3.2 reshape.410
  429.1 3.6 multiply_reduce_fusion.3
  440.5 7.1 %pad_add_fusion = f32[259,2048]{0,1:T(8,128)} fusion(f32[256,2048]{0,1:T(8,128)} %copy-done.9, f32[256,2048]{0,1:T(8,128)} %copy-done.10, f32[256,2048]{0,1:T(8,128)} %copy-done.11, f32[256,2048]{0,1:T(8,128)S(1)} %get-tuple-element.147), kind=kLoop, calls=%fused_computation.4 | loop fusion | flops 1591296 | bytes 10510336 | tf_op jit(solution)/shard_map/transpose(jvp())/add_any | solution.py:170
  448.0 2.7 fusion.5
  450.8 4.9 convolution_convert_fusion
  460.0 4.8 convolution_convert_fusion.4
  466.0 13.0 %collective-permute-done.13 = bf16[256,1024]{1,0:T(8,128)(2,1)S(1)} collective-permute-done((bf16[256,1024]{1,0:T(8,128)(2,1)S(1)}, bf16[256,1024]{1,0:T(8,128)(2,1)S(1)}, u32[]{:S(2)}, u32[]{:S(2)}) %collective-permute-start.13) | collective-permute-done | bytes 524320 | tf_op jit(solution)/shard_map/ppermute | solution.py:64
  479.6 58.4 %psum.7 = f32[10504]{0:T(1024)S(1)} all-reduce(f32[10504]{0:T(1024)S(1)} %concatenate.109), channel_id=1, replica_groups=mesh['dp'=16,'tensor'=2] {'dp'}, use_global_device_ids=true, to_apply=%region_31.32 | all-reduce | flops 10504 | bytes 84032 | tf_op jit(solution)/shard_map/psum | solution.py:408
  548.2 40.7 %reduce-scatter.7.cloned.1.call-done = bf16[64,3080]{1,0:T(8,128)(2,1)} async-done(((bf16[1024,3080]{1,0:T(8,128)(2,1)}), bf16[64,3080]{1,0:T(8,128)(2,1)}) %reduce-scatter.7.cloned.1.call-update) | async-done | bytes 394256 | tf_op jit(solution)/shard_map/reduce_scatter | solution.py:207
  (575 shorter events, 183.4 us)
Async XLA Ops:
  7.2 69.9 %all-gather.5.cloned.1.call-start = ((), (), s32[]{:S(2)}) async-start(), calls=%async_computation.4 | async-start | bytes 6963200 | tf_op jit(solution)/shard_map/all_gather | solution.py:255
  10.9 213.4 %all-gather.7.cloned.1.call-start = ((), (), s32[]{:S(2)}) async-start(), calls=%async_computation.5 | async-start | bytes 2228224 | tf_op jit(solution)/shard_map/all_gather | solution.py:268
  11.7 231.4 %all-gather.9.cloned.1.call-start = ((), (), s32[]{:S(2)}) async-start(), calls=%async_computation.6 | async-start | bytes 6127616 | tf_op jit(solution)/shard_map/all_gather | solution.py:324
  12.5 236.8 %all-gather.11.cloned.1.call-start = ((), (), s32[]{:S(2)}) async-start(), calls=%async_computation.7 | async-start | bytes 3063808 | tf_op jit(solution)/shard_map/all_gather | solution.py:327
  13.1 529.2 %reduce-scatter.9.cloned.1.call-start = ((), (), s32[]{:S(2)}) async-start(), calls=%async_computation.9 | async-start | bytes 2228224 | tf_op jit(solution)/shard_map/reduce_scatter | solution.py:207
  15.5 77.7 %copy-start.133 = (f32[256]{0:T(256)}, f32[256]{0:T(256)S(1)}, u32[]{:S(2)}) copy-start(f32[256]{0:T(256)S(1)} %get-tuple-element.194) | copy-start | bytes 3076
  15.5 77.7 %copy-start.135 = (f32[256]{0:T(256)}, f32[256]{0:T(256)S(1)}, u32[]{:S(2)}) copy-start(f32[256]{0:T(256)S(1)} %get-tuple-element.195) | copy-start | bytes 3076
  15.5 77.7 %copy-start.137 = (f32[256]{0:T(256)}, f32[256]{0:T(256)S(1)}, u32[]{:S(2)}) copy-start(f32[256]{0:T(256)S(1)} %get-tuple-element.196) | copy-start | bytes 3076
  15.5 77.7 %copy-start.139 = (f32[256]{0:T(256)}, f32[256]{0:T(256)S(1)}, u32[]{:S(2)}) copy-start(f32[256]{0:T(256)S(1)} %get-tuple-element.197) | copy-start | bytes 3076
  15.6 67.3 %copy-start.108 = (f32[1,1024]{1,0:T(1,128)}, f32[1,1024]{1,0:T(1,128)S(1)}, u32[]{:S(2)}) copy-start(f32[1,1024]{1,0:T(1,128)S(1)} %get-tuple-element.187) | copy-start | bytes 12292
  15.8 67.1 %copy-start.143 = (f32[256]{0:T(256)}, f32[256]{0:T(256)S(1)}, u32[]{:S(2)}) copy-start(f32[256]{0:T(256)S(1)} %add_rsqrt_fusion.3) | copy-start | bytes 3076
  15.9 77.3 %copy-start.100 = (f32[1,2048]{1,0:T(1,128)}, f32[1,2048]{1,0:T(1,128)S(1)}, u32[]{:S(2)}) copy-start(f32[1,2048]{1,0:T(1,128)S(1)} %get-tuple-element.182) | copy-start | bytes 24580
  15.9 77.3 %copy-start.102 = (f32[1,2048]{1,0:T(1,128)}, f32[1,2048]{1,0:T(1,128)S(1)}, u32[]{:S(2)}) copy-start(f32[1,2048]{1,0:T(1,128)S(1)} %get-tuple-element.183) | copy-start | bytes 24580
  15.9 77.3 %copy-start.104 = (f32[1,2048]{1,0:T(1,128)}, f32[1,2048]{1,0:T(1,128)S(1)}, u32[]{:S(2)}) copy-start(f32[1,2048]{1,0:T(1,128)S(1)} %get-tuple-element.184) | copy-start | bytes 24580
  15.9 77.3 %copy-start.106 = (f32[1,2048]{1,0:T(1,128)}, f32[1,2048]{1,0:T(1,128)S(1)}, u32[]{:S(2)}) copy-start(f32[1,2048]{1,0:T(1,128)S(1)} %get-tuple-element.185) | copy-start | bytes 24580
  15.9 70.1 %copy-start.158 = (f32[4]{0:T(128)}, f32[4]{0:T(128)S(1)}, u32[]{:S(2)}) copy-start(f32[4]{0:T(128)S(1)} %exponential_negate_fusion) | copy-start | bytes 52
  83.1 8.1 %collective-permute-start = (bf16[3,2048]{0,1:T(8,128)(2,1)S(1)}, bf16[3,2048]{0,1:T(8,128)(2,1)}, u32[]{:S(2)}, u32[]{:S(2)}) collective-permute-start(bf16[3,2048]{0,1:T(8,128)(2,1)S(1)} %slice.342), channel_id=1, source_target_pairs={{0,2},{2,4},{4,6},{6,8},{8,10},{10,12},{12,14},{14,16},{16,18},{18... | collective-permute-start | bytes 36872 | tf_op jit(solution)/shard_map/ppermute | solution.py:19
  139.4 17.9 %copy-start.29 = (f32[4,128,384]{2,1,0:T(8,128)}, f32[4,128,384]{2,1,0:T(8,128)S(1)}, u32[]{:S(2)}) copy-start(f32[4,128,384]{2,1,0:T(8,128)S(1)} %convolution_add_fusion.7) | copy-start | bytes 2359300
  139.4 37.2 %copy-start.163 = (bf16[256]{0:T(256)(128)(2,1)S(1)}, bf16[256]{0:T(256)(128)(2,1)}, u32[]{:S(2)}) copy-start(bf16[256]{0:T(256)(128)(2,1)} %param.26) | copy-start | bytes 1540
  140.0 5.3 collective-permute-start.1
  145.2 10.8 %collective-permute-start.2 = (bf16[4,128,384]{2,1,0:T(8,128)(2,1)S(1)}, bf16[4,128,384]{2,1,0:T(8,128)(2,1)S(1)}, u32[]{:S(2)}, u32[]{:S(2)}) collective-permute-start(bf16[4,128,384]{2,1,0:T(8,128)(2,1)S(1)} %collective-permute-done.1), channel_id=1, source_target_pairs={{0,2},{2,4},{4,6},{6,8},{8,10},{10,12},{12,14},{14,16},{16,18},{18... | collective-permute-start | bytes 1179656 | tf_op jit(solution)/shard_map/ppermute | solution.py:19
  157.3 24.1 %collective-permute-start.3 = (bf16[4,128,384]{2,1,0:T(8,128)(2,1)}, bf16[4,128,384]{2,1,0:T(8,128)(2,1)}, u32[]{:S(2)}, u32[]{:S(2)}) collective-permute-start(bf16[4,128,384]{2,1,0:T(8,128)(2,1)} %get-tuple-element.200), channel_id=1, source_target_pairs={{0,4},{2,6},{4,8},{6,10},{8,12},{10,14},{12,16},{14,18},{16,20},{1... | collective-permute-start | bytes 1179656 | tf_op jit(solution)/shard_map/ppermute | solution.py:19
  178.8 18.7 %copy-start.51 = (f32[4,128,256]{2,1,0:T(8,128)S(1)}, f32[4,128,256]{2,1,0:T(8,128)}, u32[]{:S(2)}) copy-start(f32[4,128,256]{2,1,0:T(8,128)} %get-tuple-element.145) | copy-start | bytes 1572868
  178.8 18.7 %copy-start.71 = (f32[4,128,128]{2,1,0:T(8,128)S(1)}, f32[4,128,128]{2,1,0:T(8,128)}, u32[]{:S(2)}) copy-start(f32[4,128,128]{2,1,0:T(8,128)} %copy.462) | copy-start | bytes 786436
  180.0 17.5 %copy-start.1 = (f32[4,4,64,384]{3,2,1,0:T(8,128)S(1)}, f32[4,4,64,384]{3,2,1,0:T(8,128)}, u32[]{:S(2)}) copy-start(f32[4,4,64,384]{3,2,1,0:T(8,128)} %copy-done) | copy-start | bytes 4718596
  180.1 17.6 %copy-start.58 = (bf16[256,4,128]{2,0,1:T(8,128)(2,1)S(1)}, bf16[256,4,128]{2,0,1:T(8,128)(2,1)}, u32[]{:S(2)}) copy-start(bf16[256,4,128]{2,0,1:T(8,128)(2,1)} %copy-done.57) | copy-start | bytes 786436
  180.1 17.6 %copy-start.97 = (f32[4,4,64]{2,1,0:T(4,128)S(1)}, f32[4,4,64]{2,1,0:T(4,128)}, u32[]{:S(2)}) copy-start(f32[4,4,64]{2,1,0:T(4,128)} %copy.457) | copy-start | bytes 12292
  182.9 24.8 %copy-start.28 = (f32[4,128,384]{2,1,0:T(8,128)S(1)}, f32[4,128,384]{2,1,0:T(8,128)}, u32[]{:S(2)}) copy-start(f32[4,128,384]{2,1,0:T(8,128)} %copy-done.27) | copy-start | bytes 2359300
  182.9 24.8 %copy-start.30 = (f32[4,128,384]{2,1,0:T(8,128)S(1)}, f32[4,128,384]{2,1,0:T(8,128)}, u32[]{:S(2)}) copy-start(f32[4,128,384]{2,1,0:T(8,128)} %copy-done.29) | copy-start | bytes 2359300
  182.9 24.5 %collective-permute-start.4 = (bf16[4,128,256]{2,1,0:T(8,128)(2,1)S(1)}, bf16[4,128,256]{2,1,0:T(8,128)(2,1)S(1)}, u32[]{:S(2)}, u32[]{:S(2)}) collective-permute-start(bf16[4,128,256]{2,1,0:T(8,128)(2,1)S(1)} %slice.544), channel_id=1, source_target_pairs={{0,8},{2,10},{4,12},{6,14},{8,16},{10,18},{12,20},{14,22},{16,24},... | collective-permute-start | bytes 786440 | tf_op jit(solution)/shard_map/ppermute | solution.py:19
  224.3 17.0 %copy-start.19 = (bf16[256,1024]{1,0:T(8,128)(2,1)S(1)}, bf16[256,1024]{1,0:T(8,128)(2,1)}, u32[]{:S(2)}) copy-start(bf16[256,1024]{1,0:T(8,128)(2,1)} %param.15) | copy-start | bytes 1572868
  226.9 14.4 %collective-permute-start.5 = (bf16[256,1024]{1,0:T(8,128)(2,1)S(1)}, bf16[256,1024]{1,0:T(8,128)(2,1)S(1)}, u32[]{:S(2)}, u32[]{:S(2)}) collective-permute-start(bf16[256,1024]{1,0:T(8,128)(2,1)S(1)} %convolution_convert_fusion.6), channel_id=1, source_target_pairs={{0,1},{1,0},{2,3},{3,2},{4,5},{5,4},{6,7},{7,6},{8,9},{9,8},{10,11... | collective-permute-start | bytes 1572872 | tf_op jit(solution)/shard_map/ppermute | solution.py:64
  255.5 14.9 %collective-permute-start.7 = (bf16[256,1024]{1,0:T(8,128)(2,1)S(1)}, bf16[256,1024]{1,0:T(8,128)(2,1)S(1)}, u32[]{:S(2)}, u32[]{:S(2)}) collective-permute-start(bf16[256,1024]{1,0:T(8,128)(2,1)S(1)} %convolution_convert_fusion.7), channel_id=1, source_target_pairs={{0,1},{1,0},{2,3},{3,2},{4,5},{5,4},{6,7},{7,6},{8,9},{9,8},{10,11... | collective-permute-start | bytes 1572872 | tf_op jit(solution)/shard_map/ppermute | solution.py:64
  258.2 22.2 %copy-start.73 = (bf16[256,1024]{1,0:T(8,128)(2,1)S(1)}, bf16[256,1024]{1,0:T(8,128)(2,1)}, u32[]{:S(2)}) copy-start(bf16[256,1024]{1,0:T(8,128)(2,1)} %param.16) | copy-start | bytes 1572868
  258.2 22.2 %collective-permute-start.6 = (bf16[256,1024]{1,0:T(8,128)(2,1)S(1)}, bf16[256,1024]{1,0:T(8,128)(2,1)S(1)}, u32[]{:S(2)}, u32[]{:S(2)}) collective-permute-start(bf16[256,1024]{1,0:T(8,128)(2,1)S(1)} %convolution_convert_fusion.5), channel_id=1, source_target_pairs={{0,1},{1,0},{2,3},{3,2},{4,5},{5,4},{6,7},{7,6},{8,9},{9,8},{10,11... | collective-permute-start | bytes 1572872 | tf_op jit(solution)/shard_map/ppermute | solution.py:64
  284.8 259.1 %reduce-scatter.13.cloned.1.call-start = ((), (), s32[]{:S(2)}) async-start(), calls=%async_computation.11 | async-start | bytes 3063808
  295.5 250.5 %reduce-scatter.11.cloned.1.call-start = ((), (), s32[]{:S(2)}) async-start(), calls=%async_computation.10 | async-start | bytes 6127616 | tf_op jit(solution)/shard_map/reduce_scatter | solution.py:207
  324.7 3.6 collective-permute-start.8
  328.3 7.3 %collective-permute-start.9 = (bf16[4,128,384]{2,1,0:T(8,128)(2,1)S(1)}, bf16[4,128,384]{2,1,0:T(8,128)(2,1)S(1)}, u32[]{:S(2)}, u32[]{:S(2)}) collective-permute-start(bf16[4,128,384]{2,1,0:T(8,128)(2,1)S(1)} %collective-permute-done.8), channel_id=1, source_target_pairs={{2,0},{4,2},{6,4},{8,6},{10,8},{12,10},{14,12},{16,14},{18,16},{20... | collective-permute-start | bytes 1179656 | tf_op jit(solution)/shard_map/ppermute | solution.py:19
  336.9 13.7 %collective-permute-start.10 = (bf16[4,128,384]{2,1,0:T(8,128)(2,1)}, bf16[4,128,384]{2,1,0:T(8,128)(2,1)}, u32[]{:S(2)}, u32[]{:S(2)}) collective-permute-start(bf16[4,128,384]{2,1,0:T(8,128)(2,1)} %get-tuple-element.206), channel_id=1, source_target_pairs={{4,0},{6,2},{8,4},{10,6},{12,8},{14,10},{16,12},{18,14},{20,16},{2... | collective-permute-start | bytes 1179656 | tf_op jit(solution)/shard_map/ppermute | solution.py:19
  342.5 246.5 %reduce-scatter.7.cloned.1.call-start = ((), (), s32[]{:S(2)}) async-start(), calls=%async_computation.8 | async-start | bytes 6963200 | tf_op jit(solution)/shard_map/reduce_scatter | solution.py:207
  352.0 16.4 %collective-permute-start.11 = (bf16[4,128,256]{2,1,0:T(8,128)(2,1)S(1)}, bf16[4,128,256]{2,1,0:T(8,128)(2,1)S(1)}, u32[]{:S(2)}, u32[]{:S(2)}) collective-permute-start(bf16[4,128,256]{2,1,0:T(8,128)(2,1)S(1)} %slice.543), channel_id=1, source_target_pairs={{8,0},{10,2},{12,4},{14,6},{16,8},{18,10},{20,12},{22,14},{24,16},... | collective-permute-start | bytes 786440 | tf_op jit(solution)/shard_map/ppermute | solution.py:19
  356.2 13.4 %copy-start.64 = (f32[4,4,128,128]{3,2,1,0:T(8,128)}, f32[4,4,128,128]{3,2,1,0:T(8,128)S(1)}, u32[]{:S(2)}) copy-start(f32[4,4,128,128]{3,2,1,0:T(8,128)S(1)} %fusion.8) | copy-start | bytes 3145732
  438.0 9.6 %collective-permute-start.12 = (f32[3,2048]{1,0:T(4,128)S(1)}, f32[3,2048]{1,0:T(4,128)S(1)}, u32[]{:S(2)}, u32[]{:S(2)}) collective-permute-start(f32[3,2048]{1,0:T(4,128)S(1)} %copy.491), channel_id=1, source_target_pairs={{2,0},{4,2},{6,4},{8,6},{10,8},{12,10},{14,12},{16,14},{18,16},{20... | collective-permute-start | bytes 73736 | tf_op jit(solution)/shard_map/ppermute | solution.py:19
  456.4 3.6 collective-permute-start.14
  460.0 19.5 %copy-start.141 = (f32[1024]{0:T(1024)S(1)}, f32[1024]{0:T(1024)}, u32[]{:S(2)}) copy-start(f32[1024]{0:T(1024)} %get-tuple-element.118) | copy-start | bytes 12292
  464.8 76.1 %copy-start.15 = (f32[256,1024]{1,0:T(8,128)S(1)}, f32[256,1024]{1,0:T(8,128)}, u32[]{:S(2)}) copy-start(f32[256,1024]{1,0:T(8,128)} %copy-done.14) | copy-start | bytes 3145732
  464.9 14.2 %collective-permute-start.13 = (bf16[256,1024]{1,0:T(8,128)(2,1)S(1)}, bf16[256,1024]{1,0:T(8,128)(2,1)S(1)}, u32[]{:S(2)}, u32[]{:S(2)}) collective-permute-start(bf16[256,1024]{1,0:T(8,128)(2,1)S(1)} %convolution_convert_fusion.4), channel_id=1, source_target_pairs={{0,1},{1,0},{2,3},{3,2},{4,5},{5,4},{6,7},{7,6},{8,9},{9,8},{10,11... | collective-permute-start | bytes 1572872 | tf_op jit(solution)/shard_map/ppermute | solution.py:64
  (142 other events, 590.6 us)
Sparse Core Ops, SparseCore 0:
  11.0 66.0 all-gather.4
  79.3 40.6 all-gather.6
  122.8 61.7 all-gather.8
  186.8 45.3 all-gather.10
  285.0 61.2 reduce-scatter.8
  350.4 63.8 reduce-scatter.12
  418.2 80.7 reduce-scatter.10
  502.9 86.0 reduce-scatter.6

commit v2 on v1

--- a/solution.py
+++ b/solution.py
@@ -200,6 +200,82 @@
     return lax.dot_general(
         left, right, (((1,), (1,)), ((), ())), preferred_element_type=jnp.float32
     )
+
+
+def ring_place(axis):
+    chips = lax.axis_size(axis) // 2
+    cycle = list(range(0, chips, 2)) + list(range(1, chips, 2))[::-1]
+    orders = [cycle, cycle[::-1]]
+    route = []
+    for core in range(2):
+        for i in range(chips):
+            source, target = orders[core][i], orders[core][(i + 1) % chips]
+            route.append((2 * source + core, 2 * target + core))
+    mine = lax.axis_index(axis)
+    core = mine % 2
+    places = [[order.index(chip) for chip in range(chips)] for order in orders]
+    place = jnp.asarray(places, jnp.int32)[core, mine // 2]
+
+    def chip_behind(back):
+        return jnp.asarray(orders, jnp.int32)[core, (place - back) % chips]
+
+    return route, core, chip_behind
+
+
+def uses_ring(axis):
+    size = lax.axis_size(axis)
+    return size % 4 == 0 and 4 <= size <= 16
+
+
+def gathered_rows(part, axis):
+    if not uses_ring(axis):
+        return lax.all_gather(part, axis, axis=0, tiled=True)
+    size = lax.axis_size(axis)
+    route, core, chip_behind = ring_place(axis)
+    held = jnp.zeros((size // 2,) + part.shape, part.dtype)
+    moving = part
+    for step in range(size // 2):
+        if step:
+            moving = lax.ppermute(moving, axis, route)
+        held = lax.dynamic_update_index_in_dim(held, moving, chip_behind(step), 0)
+    other = lax.ppermute(held, axis, [(i, i ^ 1) for i in range(size)])
+    first = core == 0
+    both = jnp.stack([jnp.where(first, held, other), jnp.where(first, other, held)], axis=1)
+    return both.reshape(size * part.shape[0], part.shape[1])
+
+
+def scattered_rows(part, axis):
+    if not uses_ring(axis):
+        return lax.psum_scatter(part, axis, scatter_dimension=0, tiled=True)
+    size = lax.axis_size(axis)
+    route, core, chip_behind = ring_place(axis)
+    cut = part.reshape(size // 2, 2, part.shape[0] // size, part.shape[1])
+    other = lax.ppermute(
+        lax.dynamic_index_in_dim(cut, 1 - core, 1, keepdims=False),
+        axis,
+        [(i, i ^ 1) for i in range(size)],
+    )
+    own = lax.dynamic_index_in_dim(cut, core, 1, keepdims=False)
+    pair = (own.astype(jnp.float32) + other.astype(jnp.float32)).astype(part.dtype)
+    moving = lax.dynamic_index_in_dim(pair, chip_behind(1), 0, keepdims=False)
+    for step in range(1, size // 2):
+        moving = lax.ppermute(moving, axis, route).astype(jnp.float32)
+        mine = lax.dynamic_index_in_dim(pair, chip_behind(1 + step), 0, keepdims=False)
+        moving = moving + mine.astype(jnp.float32)
+        if step < size // 2 - 1:
+            moving = moving.astype(part.dtype)
+    return moving
+
+
+def doubled_sum(values, axis):
+    size = lax.axis_size(axis)
+    if size & (size - 1):
+        return lax.psum(values, axis)
+    distance = 1
+    while distance < size:
+        values = values + lax.ppermute(values, axis, [(i, i ^ distance) for i in range(size)])
+        distance = 2 * distance
+    return values
 
 
 def summed_rows(left, right):
@@ -252,7 +328,7 @@
     scale_one = lax.rsqrt(jnp.mean(inputs * inputs, axis=-1, keepdims=True) + 1e-06)
     unit_one = inputs * scale_one
     normed = (unit_one * gains[0]).astype(jnp.bfloat16)
-    full_in = lax.all_gather(
+    full_in = gathered_rows(
         jnp.concatenate(
             [
                 query_key_weight.reshape(-1, 2 * width_k),
@@ -262,8 +338,6 @@
             axis=1,
         ),
         "dp",
-        axis=0,
-        tiled=True,
     )
     full_out = lax.all_gather(out_weight, "dp", axis=0, tiled=True)
     width_c = 2 * width_k + width_v
@@ -391,7 +465,9 @@
     grad_in_low = jnp.concatenate(
         [grad_pre_low, grad_gate_raw.astype(jnp.bfloat16), grad_ab.astype(jnp.bfloat16)], axis=1
     )
-    share_in = summed_rows(normed, grad_in_low)
+    share_in = scattered_rows(
+        contract_rows(normed, grad_in_low).astype(jnp.bfloat16), "dp"
+    ).astype(jnp.float32)
     grad_normed = pair_sum(contract_cols(grad_in_low, full_in).astype(jnp.bfloat16), "tensor")
     grad_gain_out = pair_sum(grad_gain_part, "tensor")
     gain_one_grad = jnp.sum(grad_normed * unit_one, axis=0)
@@ -405,7 +481,7 @@
         grad_decay_log,
         grad_decay_bias,
     )
-    small = lax.psum(jnp.concatenate(small_parts), "dp")
+    small = doubled_sum(jnp.concatenate(small_parts), "dp")
     sums = []
     at = 0
     for part in small_parts:

time: 609 us -> 687 us (1.13)
  blocking collectives: 58.4 us -> 0 us
  between operations: 16.9 us -> 59.8 us
  starting transfers between devices: 63.5 us -> 95.1 us
  local copies, waits for them, and re-layouts: 109 us -> 139 us
  other arithmetic: 73.2 us -> 91.3 us
  waiting for transfers between devices: 190 us -> 204 us
    ppermute x0 -> x20, waiting for transfers between devices: none -> 84.6 us  [the longest x7 57.5 us: gathered_rows(): moving = lax.ppermute(moving, axis, route)]
    all_gather x1 -> x0, waiting for transfers between devices: 59.7 us -> none  [local(): lax.all_gather(jnp.concatenate([query_key_weight.reshape(-1, 2 * width_k)...]
    psum x1 -> x0, blocking collectives: 58.4 us -> none  [local(): small = lax.psum(jnp.concatenate(small_parts), 'dp')]
    ppermute x0 -> x20, starting transfers between devices: none -> 41.1 us  [the longest x7 23.2 us: gathered_rows(): moving = lax.ppermute(moving, axis, route)]
    ppermute x5, waiting for transfers between devices: 49.1 us -> 31.6 us  [pair_sum(): other = lax.ppermute(part, axis, [(0, 1), (1, 0)])]
    reduce_scatter x3 -> x2, waiting for transfers between devices: 40.7 us -> 55.5 us  [summed_rows(): share = lax.psum_scatter(part, 'dp', scatter_dimension=0, tiled=True)]
    squeeze x2, local copies, waits for them, and re-layouts: 2.97 us -> 14.9 us  [local(): maps = [jnp.concatenate([kept_a[0], step_b[0]], axis=-1)]]
    convert_element_type x0 -> x7, other arithmetic: none -> 10.6 us  [the longest x6 6.73 us: scattered_rows(): moving = moving.astype(part.dtype)]
  transfers between devices with their start and end apart: 23 -> 41, of which waited for: 15 -> 26; matrix products, arithmetic and copies ran while one was open for 40% -> 39% of each run, Pallas kernels for 0% -> 0%
where the time goes in v2:
time: 687 us; the launch traced here: 677 us
  waiting for transfers between devices  204 us (30%)
  local copies, waits for them, and re-layouts  139 us (20%)
  starting transfers between devices  95.1 us (14%)
  other arithmetic  91.3 us (13%)
  matrix products  87.5 us (13%)
  between operations  59.8 us (9%)
    ppermute x7, waiting for transfers between devices, gathered_rows(): moving = lax.ppermute(moving, axis, route)  57.5 us
    reduce_scatter x2, waiting for transfers between devices, summed_rows(): share = lax.psum_scatter(part, 'dp', scatter_dimension=0, tiled=True)  55.5 us
    ppermute x10, starting transfers between devices, shifted(): return lax.ppermute(block, axis, route)  46.9 us
    ppermute x10, waiting for transfers between devices, shifted(): return lax.ppermute(block, axis, route)  31.6 us
    ppermute x5, waiting for transfers between devices, pair_sum(): other = lax.ppermute(part, axis, [(0, 1), (1, 0)])  31.6 us
    unnamed x375, local copies, waits for them, and re-layouts  27.5 us
    dot_general x27, matrix products, matmul(): return jnp.einsum('...ij,...jk->...ik', left, right, precision=accuracy)  27 us
    ppermute x7, starting transfers between devices, gathered_rows(): moving = lax.ppermute(moving, axis, route)  23.2 us
  transfers between devices with their start and end apart: 41, of which 26 were waited for; matrix products, arithmetic and copies ran while one was open for 39% of the time, Pallas kernels for 0%

profile of v2, /device:TPU:0, one launch (start us, length us, event | category | flops | bytes accessed | tf_op | source)
XLA Modules:
  0.0 676.6 jit_solution(2075329040350771754)
XLA Ops:
  12.6 3.1 collective-permute-start
  47.2 6.3 collective-permute-done.1
  55.9 6.1 collective-permute-done.2
  63.9 13.8 %collective-permute-done.3 = bf16[64,3080]{1,0:T(8,128)(2,1)S(1)} collective-permute-done((bf16[64,3080]{1,0:T(8,128)(2,1)S(1)}, bf16[64,3080]{1,0:T(8,128)(2,1)S(1)}, u32[]{:S(2)}, u32[]{:S(2)}) %collective-permute-start.3) | collective-permute-done | bytes 394272 | tf_op jit(solution)/shard_map/ppermute | solution.py:239
  77.7 4.8 collective-permute-start.4
  82.5 5.4 collective-permute-done.4
  87.9 3.5 collective-permute-start.5
  91.4 14.2 %collective-permute-done.5 = bf16[64,3080]{1,0:T(8,128)(2,1)S(1)} collective-permute-done((bf16[64,3080]{1,0:T(8,128)(2,1)S(1)}, bf16[64,3080]{1,0:T(8,128)(2,1)S(1)}, u32[]{:S(2)}, u32[]{:S(2)}) %collective-permute-start.5) | collective-permute-done | bytes 394272 | tf_op jit(solution)/shard_map/ppermute | solution.py:239
  105.6 6.0 collective-permute-start.6
  111.7 11.7 %collective-permute-done.6 = bf16[64,3080]{1,0:T(8,128)(2,1)S(1)} collective-permute-done((bf16[64,3080]{1,0:T(8,128)(2,1)S(1)}, bf16[64,3080]{1,0:T(8,128)(2,1)S(1)}, u32[]{:S(2)}, u32[]{:S(2)}) %collective-permute-start.6) | collective-permute-done | bytes 394272 | tf_op jit(solution)/shard_map/ppermute | solution.py:239
  143.8 4.3 fusion.7
  185.1 13.1 %slice_bitcast_fusion.15 = f32[4,128,128]{1,2,0:T(8,128)} fusion(f32[4,4,128,128]{2,3,1,0:T(8,128)S(1)} %subtract_multiply_fusion.2), kind=kLoop, calls=%fused_computation.259 | loop fusion | bytes 524288 | tf_op jit(solution)/shard_map/squeeze | solution.py:372
  203.2 4.6 collective-permute-start.9
  209.2 7.8 %collective-permute-start.10 = (bf16[4,128,384]{2,1,0:T(8,128)(2,1)S(1)}, bf16[4,128,384]{2,1,0:T(8,128)(2,1)S(1)}, u32[]{:S(2)}, u32[]{:S(2)}) collective-permute-start(bf16[4,128,384]{2,1,0:T(8,128)(2,1)S(1)} %collective-permute-done.9), channel_id=1, source_target_pairs={{0,2},{2,4},{4,6},{6,8},{8,10},{10,12},{12,14},{14,16},{16,18},{18... | collective-permute-start | bytes 1179656 | tf_op jit(solution)/shard_map/ppermute | solution.py:19
  219.5 10.9 %collective-permute-start.11 = (bf16[4,128,384]{2,1,0:T(8,128)(2,1)}, bf16[4,128,384]{2,1,0:T(8,128)(2,1)}, u32[]{:S(2)}, u32[]{:S(2)}) collective-permute-start(bf16[4,128,384]{2,1,0:T(8,128)(2,1)} %get-tuple-element.232), channel_id=1, source_target_pairs={{0,4},{2,6},{4,8},{6,10},{8,12},{10,14},{12,16},{14,18},{16,20},{1... | collective-permute-start | bytes 1179656 | tf_op jit(solution)/shard_map/ppermute | solution.py:19
  236.8 14.1 %collective-permute-start.12 = (bf16[4,128,256]{2,1,0:T(8,128)(2,1)S(1)}, bf16[4,128,256]{2,1,0:T(8,128)(2,1)S(1)}, u32[]{:S(2)}, u32[]{:S(2)}) collective-permute-start(bf16[4,128,256]{2,1,0:T(8,128)(2,1)S(1)} %slice.544), channel_id=1, source_target_pairs={{0,8},{2,10},{4,12},{6,14},{8,16},{10,18},{12,20},{14,22},{16,24},... | collective-permute-start | bytes 786440 | tf_op jit(solution)/shard_map/ppermute | solution.py:19
  251.2 3.5 collective-permute-done.12
  262.7 3.2 reshape.457
  277.3 8.3 %collective-permute-done.13 = bf16[256,1024]{1,0:T(8,128)(2,1)S(1)} collective-permute-done((bf16[256,1024]{1,0:T(8,128)(2,1)S(1)}, bf16[256,1024]{1,0:T(8,128)(2,1)S(1)}, u32[]{:S(2)}, u32[]{:S(2)}) %collective-permute-start.13) | collective-permute-done | bytes 524320 | tf_op jit(solution)/shard_map/ppermute | solution.py:64
  287.4 6.3 fusion.218
  293.7 4.3 multiply_convert_fusion.1
  304.9 10.0 %collective-permute-done.15 = bf16[256,1024]{1,0:T(8,128)(2,1)S(1)} collective-permute-done((bf16[256,1024]{1,0:T(8,128)(2,1)S(1)}, bf16[256,1024]{1,0:T(8,128)(2,1)S(1)}, u32[]{:S(2)}, u32[]{:S(2)}) %collective-permute-start.15) | collective-permute-done | bytes 524320 | tf_op jit(solution)/shard_map/ppermute | solution.py:64
  315.9 5.5 collective-permute-done.14
  330.5 3.4 fusion.43
  333.9 3.2 reshape.463
  337.1 3.1 copy.581
  340.2 3.3 multiply_reduce_fusion.4
  359.1 6.4 collective-permute-done.17
  373.4 10.9 %collective-permute-done.18 = bf16[4,128,384]{2,1,0:T(8,128)(2,1)} collective-permute-done((bf16[4,128,384]{2,1,0:T(8,128)(2,1)}, bf16[4,128,384]{2,1,0:T(8,128)(2,1)}, u32[]{:S(2)}, u32[]{:S(2)}) %collective-permute-start.18) | collective-permute-done | bytes 393248 | tf_op jit(solution)/shard_map/ppermute | solution.py:19
  393.9 4.3 collective-permute-done.19
  408.3 3.1 multiply_reduce_fusion.13
  427.3 3.3 multiply_bitcast_fusion
  458.3 3.2 reshape.458
  464.0 4.2 multiply_reduce_fusion.3
  475.8 7.0 %pad_add_fusion = f32[259,2048]{0,1:T(8,128)} fusion(f32[256,2048]{0,1:T(8,128)} %copy-done.12, f32[256,2048]{0,1:T(8,128)} %copy-done.13, f32[256,2048]{0,1:T(8,128)} %copy-done.14, f32[256,2048]{0,1:T(8,128)S(1)} %get-tuple-element.163), kind=kLoop, calls=%fused_computation.10 | loop fusion | flops 1591296 | bytes 10510336 | tf_op jit(solution)/shard_map/transpose(jvp())/add_any | solution.py:170
  487.0 4.6 convolution_convert_fusion
  491.6 9.4 %copy.614 = bf16[1024,3080]{1,0:T(8,128)(2,1)} copy(bf16[1024,3080]{0,1:T(8,128)(2,1)} %convolution_convert_fusion) | data formatting | bytes 12615680 | tf_op jit(solution)/shard_map/convert_element_type | solution.py:469
  500.9 4.0 dynamic-slice_bitcast_fusion
  507.0 3.0 copy.655
  513.6 3.8 fusion
  518.3 4.2 collective-permute-start.28
  522.5 4.4 convolution_convert_fusion.1
  542.2 12.0 %collective-permute-done.30 = bf16[64,3080]{1,0:T(8,128)(2,1)S(1)} collective-permute-done((bf16[64,3080]{1,0:T(8,128)(2,1)S(1)}, bf16[64,3080]{1,0:T(8,128)(2,1)S(1)}, u32[]{:S(2)}, u32[]{:S(2)}) %collective-permute-start.30) | collective-permute-done | bytes 394272 | tf_op jit(solution)/shard_map/ppermute | solution.py:262
  554.7 4.9 convolution_convert_fusion.4
  561.3 3.2 collective-permute-done.31
  565.9 7.9 %collective-permute-done.21 = bf16[256,1024]{1,0:T(8,128)(2,1)S(1)} collective-permute-done((bf16[256,1024]{1,0:T(8,128)(2,1)S(1)}, bf16[256,1024]{1,0:T(8,128)(2,1)S(1)}, u32[]{:S(2)}, u32[]{:S(2)}) %collective-permute-start.21) | collective-permute-done | bytes 524320 | tf_op jit(solution)/shard_map/ppermute | solution.py:64
  593.0 4.6 collective-permute-done.33
  611.5 55.5 %reduce-scatter.8.cloned.1.call-done = bf16[64,2816]{1,0:T(8,128)(2,1)} async-done(((bf16[1024,2816]{1,0:T(8,128)(2,1)}), bf16[64,2816]{1,0:T(8,128)(2,1)}) %reduce-scatter.8.cloned.1.call-update) | async-done | bytes 360464 | tf_op jit(solution)/shard_map/reduce_scatter | solution.py:283
  (665 shorter events, 269.4 us)
Async XLA Ops:
  7.2 32.4 %copy-start.177 = (s32[4]{0:T(128)S(1)}, s32[4]{0:T(128)}, u32[]{:S(2)}) copy-start(s32[4]{0:T(128)} %param.35) | copy-start | bytes 52
  7.2 32.5 %copy-start.167 = (bf16[4,2,512]{2,1,0:T(2,128)(2,1)S(1)}, bf16[4,2,512]{2,1,0:T(2,128)(2,1)}, u32[]{:S(2)}) copy-start(bf16[4,2,512]{2,1,0:T(2,128)(2,1)} %param.40) | copy-start | bytes 24580
  7.2 264.6 %all-gather.4.cloned.1.call-start = ((), (), s32[]{:S(2)}) async-start(), calls=%async_computation.3 | async-start | bytes 2228224 | tf_op jit(solution)/shard_map/all_gather | solution.py:342
  8.0 279.5 %all-gather.6.cloned.1.call-start = ((), (), s32[]{:S(2)}) async-start(), calls=%async_computation.4 | async-start | bytes 6127616 | tf_op jit(solution)/shard_map/all_gather | solution.py:398
  9.8 283.9 %all-gather.8.cloned.1.call-start = ((), (), s32[]{:S(2)}) async-start(), calls=%async_computation.5 | async-start | bytes 3063808 | tf_op jit(solution)/shard_map/all_gather | solution.py:401
  12.6 32.9 %collective-permute-start = (bf16[64,3080]{1,0:T(8,128)(2,1)S(1)}, bf16[64,3080]{1,0:T(8,128)(2,1)S(1)}, u32[]{:S(2)}, u32[]{:S(2)}) collective-permute-start(bf16[64,3080]{1,0:T(8,128)(2,1)S(1)} %pad_maximum_fusion.27), channel_id=1, source_target_pairs={{0,8},{8,16},{16,24},{24,28},{28,20},{20,12},{12,4},{4,0},{6,14},{... | collective-permute-start | bytes 1182728 | tf_op jit(solution)/shard_map/ppermute | solution.py:239
  15.7 588.1 %reduce-scatter.6.cloned.1.call-start = ((), (), s32[]{:S(2)}) async-start(), calls=%async_computation.6 | async-start | bytes 2228224 | tf_op jit(solution)/shard_map/reduce_scatter | solution.py:283
  45.5 8.0 %collective-permute-start.1 = (bf16[64,3080]{1,0:T(8,128)(2,1)S(1)}, bf16[64,3080]{1,0:T(8,128)(2,1)S(1)}, u32[]{:S(2)}, u32[]{:S(2)}) collective-permute-start(bf16[64,3080]{1,0:T(8,128)(2,1)S(1)} %collective-permute-done), channel_id=1, source_target_pairs={{0,8},{8,16},{16,24},{24,28},{28,20},{20,12},{12,4},{4,0},{6,14},{... | collective-permute-start | bytes 1182728 | tf_op jit(solution)/shard_map/ppermute | solution.py:239
  53.5 8.5 %collective-permute-start.2 = (bf16[64,3080]{1,0:T(8,128)(2,1)S(1)}, bf16[64,3080]{1,0:T(8,128)(2,1)S(1)}, u32[]{:S(2)}, u32[]{:S(2)}) collective-permute-start(bf16[64,3080]{1,0:T(8,128)(2,1)S(1)} %collective-permute-done.1), channel_id=1, source_target_pairs={{0,8},{8,16},{16,24},{24,28},{28,20},{20,12},{12,4},{4,0},{6,14},{... | collective-permute-start | bytes 1182728 | tf_op jit(solution)/shard_map/ppermute | solution.py:239
  55.9 69.8 %copy-start.22 = (bf16[256,1024]{1,0:T(8,128)(2,1)S(1)}, bf16[256,1024]{1,0:T(8,128)(2,1)}, u32[]{:S(2)}) copy-start(bf16[256,1024]{1,0:T(8,128)(2,1)} %param.33) | copy-start | bytes 1572868
  62.0 15.7 %collective-permute-start.3 = (bf16[64,3080]{1,0:T(8,128)(2,1)S(1)}, bf16[64,3080]{1,0:T(8,128)(2,1)S(1)}, u32[]{:S(2)}, u32[]{:S(2)}) collective-permute-start(bf16[64,3080]{1,0:T(8,128)(2,1)S(1)} %collective-permute-done.2), channel_id=1, source_target_pairs={{0,8},{8,16},{16,24},{24,28},{28,20},{20,12},{12,4},{4,0},{6,14},{... | collective-permute-start | bytes 1182728 | tf_op jit(solution)/shard_map/ppermute | solution.py:239
  63.9 62.0 %copy-start.179 = (f32[4]{0:T(128)S(1)}, f32[4]{0:T(128)}, u32[]{:S(2)}) copy-start(f32[4]{0:T(128)} %param.42) | copy-start | bytes 52
  63.9 62.6 %copy-start.156 = (bf16[2,1024]{1,0:T(2,128)(2,1)S(1)}, bf16[2,1024]{1,0:T(2,128)(2,1)}, u32[]{:S(2)}) copy-start(bf16[2,1024]{1,0:T(2,128)(2,1)} %param.36) | copy-start | bytes 12292
  63.9 62.7 %copy-start.168 = (bf16[4,1024]{1,0:T(4,128)(2,1)S(1)}, bf16[4,1024]{1,0:T(4,128)(2,1)}, u32[]{:S(2)}) copy-start(bf16[4,1024]{1,0:T(4,128)(2,1)} %param.41) | copy-start | bytes 24580
  77.7 10.2 %collective-permute-start.4 = (bf16[64,3080]{1,0:T(8,128)(2,1)S(1)}, bf16[64,3080]{1,0:T(8,128)(2,1)S(1)}, u32[]{:S(2)}, u32[]{:S(2)}) collective-permute-start(bf16[64,3080]{1,0:T(8,128)(2,1)S(1)} %collective-permute-done.3), channel_id=1, source_target_pairs={{0,8},{8,16},{16,24},{24,28},{28,20},{20,12},{12,4},{4,0},{6,14},{... | collective-permute-start | bytes 1182728 | tf_op jit(solution)/shard_map/ppermute | solution.py:239
  87.9 17.7 %collective-permute-start.5 = (bf16[64,3080]{1,0:T(8,128)(2,1)S(1)}, bf16[64,3080]{1,0:T(8,128)(2,1)S(1)}, u32[]{:S(2)}, u32[]{:S(2)}) collective-permute-start(bf16[64,3080]{1,0:T(8,128)(2,1)S(1)} %collective-permute-done.4), channel_id=1, source_target_pairs={{0,8},{8,16},{16,24},{24,28},{28,20},{20,12},{12,4},{4,0},{6,14},{... | collective-permute-start | bytes 1182728 | tf_op jit(solution)/shard_map/ppermute | solution.py:239
  105.6 17.8 %collective-permute-start.6 = (bf16[64,3080]{1,0:T(8,128)(2,1)S(1)}, bf16[64,3080]{1,0:T(8,128)(2,1)S(1)}, u32[]{:S(2)}, u32[]{:S(2)}) collective-permute-start(bf16[64,3080]{1,0:T(8,128)(2,1)S(1)} %collective-permute-done.5), channel_id=1, source_target_pairs={{0,8},{8,16},{16,24},{24,28},{28,20},{20,12},{12,4},{4,0},{6,14},{... | collective-permute-start | bytes 1182728 | tf_op jit(solution)/shard_map/ppermute | solution.py:239
  123.4 5.9 collective-permute-start.7
  133.7 8.0 %collective-permute-start.8 = (bf16[3,2048]{0,1:T(8,128)(2,1)S(1)}, bf16[3,2048]{0,1:T(8,128)(2,1)}, u32[]{:S(2)}, u32[]{:S(2)}) collective-permute-start(bf16[3,2048]{0,1:T(8,128)(2,1)S(1)} %slice.342), channel_id=1, source_target_pairs={{0,2},{2,4},{4,6},{6,8},{8,10},{10,12},{12,14},{14,16},{16,18},{18... | collective-permute-start | bytes 36872 | tf_op jit(solution)/shard_map/ppermute | solution.py:19
  203.2 6.0 collective-permute-start.9
  209.2 9.1 %collective-permute-start.10 = (bf16[4,128,384]{2,1,0:T(8,128)(2,1)S(1)}, bf16[4,128,384]{2,1,0:T(8,128)(2,1)S(1)}, u32[]{:S(2)}, u32[]{:S(2)}) collective-permute-start(bf16[4,128,384]{2,1,0:T(8,128)(2,1)S(1)} %collective-permute-done.9), channel_id=1, source_target_pairs={{0,2},{2,4},{4,6},{6,8},{8,10},{10,12},{12,14},{14,16},{16,18},{18... | collective-permute-start | bytes 1179656 | tf_op jit(solution)/shard_map/ppermute | solution.py:19
  219.5 15.7 %collective-permute-start.11 = (bf16[4,128,384]{2,1,0:T(8,128)(2,1)}, bf16[4,128,384]{2,1,0:T(8,128)(2,1)}, u32[]{:S(2)}, u32[]{:S(2)}) collective-permute-start(bf16[4,128,384]{2,1,0:T(8,128)(2,1)} %get-tuple-element.232), channel_id=1, source_target_pairs={{0,4},{2,6},{4,8},{6,10},{8,12},{10,14},{12,16},{14,18},{16,20},{1... | collective-permute-start | bytes 1179656 | tf_op jit(solution)/shard_map/ppermute | solution.py:19
  236.8 17.9 %collective-permute-start.12 = (bf16[4,128,256]{2,1,0:T(8,128)(2,1)S(1)}, bf16[4,128,256]{2,1,0:T(8,128)(2,1)S(1)}, u32[]{:S(2)}, u32[]{:S(2)}) collective-permute-start(bf16[4,128,256]{2,1,0:T(8,128)(2,1)S(1)} %slice.544), channel_id=1, source_target_pairs={{0,8},{2,10},{4,12},{6,14},{8,16},{10,18},{12,20},{14,22},{16,24},... | collective-permute-start | bytes 786440 | tf_op jit(solution)/shard_map/ppermute | solution.py:19
  274.5 11.1 %collective-permute-start.13 = (bf16[256,1024]{1,0:T(8,128)(2,1)S(1)}, bf16[256,1024]{1,0:T(8,128)(2,1)S(1)}, u32[]{:S(2)}, u32[]{:S(2)}) collective-permute-start(bf16[256,1024]{1,0:T(8,128)(2,1)S(1)} %convolution_convert_fusion.6), channel_id=1, source_target_pairs={{0,1},{1,0},{2,3},{3,2},{4,5},{5,4},{6,7},{7,6},{8,9},{9,8},{10,11... | collective-permute-start | bytes 1572872 | tf_op jit(solution)/shard_map/ppermute | solution.py:64
  299.9 14.9 %collective-permute-start.15 = (bf16[256,1024]{1,0:T(8,128)(2,1)S(1)}, bf16[256,1024]{1,0:T(8,128)(2,1)S(1)}, u32[]{:S(2)}, u32[]{:S(2)}) collective-permute-start(bf16[256,1024]{1,0:T(8,128)(2,1)S(1)} %convolution_convert_fusion.7), channel_id=1, source_target_pairs={{0,1},{1,0},{2,3},{3,2},{4,5},{5,4},{6,7},{7,6},{8,9},{9,8},{10,11... | collective-permute-start | bytes 1572872 | tf_op jit(solution)/shard_map/ppermute | solution.py:64
  302.5 18.8 %collective-permute-start.14 = (bf16[256,1024]{1,0:T(8,128)(2,1)S(1)}, bf16[256,1024]{1,0:T(8,128)(2,1)S(1)}, u32[]{:S(2)}, u32[]{:S(2)}) collective-permute-start(bf16[256,1024]{1,0:T(8,128)(2,1)S(1)} %convolution_convert_fusion.5), channel_id=1, source_target_pairs={{0,1},{1,0},{2,3},{3,2},{4,5},{5,4},{6,7},{7,6},{8,9},{9,8},{10,11... | collective-permute-start | bytes 1572872 | tf_op jit(solution)/shard_map/ppermute | solution.py:64
  350.8 3.7 collective-permute-start.16
  354.5 11.0 %collective-permute-start.17 = (bf16[4,128,384]{2,1,0:T(8,128)(2,1)}, bf16[4,128,384]{2,1,0:T(8,128)(2,1)}, u32[]{:S(2)}, u32[]{:S(2)}) collective-permute-start(bf16[4,128,384]{2,1,0:T(8,128)(2,1)} %collective-permute-done.16), channel_id=1, source_target_pairs={{2,0},{4,2},{6,4},{8,6},{10,8},{12,10},{14,12},{16,14},{18,16},{20... | collective-permute-start | bytes 1179656 | tf_op jit(solution)/shard_map/ppermute | solution.py:19
  367.8 16.5 %collective-permute-start.18 = (bf16[4,128,384]{2,1,0:T(8,128)(2,1)}, bf16[4,128,384]{2,1,0:T(8,128)(2,1)}, u32[]{:S(2)}, u32[]{:S(2)}) collective-permute-start(bf16[4,128,384]{2,1,0:T(8,128)(2,1)} %get-tuple-element.238), channel_id=1, source_target_pairs={{4,0},{6,2},{8,4},{10,6},{12,8},{14,10},{16,12},{18,14},{20,16},{2... | collective-permute-start | bytes 1179656 | tf_op jit(solution)/shard_map/ppermute | solution.py:19
  386.8 11.4 %collective-permute-start.19 = (bf16[4,128,256]{2,1,0:T(8,128)(2,1)}, bf16[4,128,256]{2,1,0:T(8,128)(2,1)}, u32[]{:S(2)}, u32[]{:S(2)}) collective-permute-start(bf16[4,128,256]{2,1,0:T(8,128)(2,1)} %slice.543), channel_id=1, source_target_pairs={{8,0},{10,2},{12,4},{14,6},{16,8},{18,10},{20,12},{22,14},{24,16},... | collective-permute-start | bytes 786440 | tf_op jit(solution)/shard_map/ppermute | solution.py:19
  392.3 213.1 %reduce-scatter.10.cloned.1.call-start = ((), (), s32[]{:S(2)}) async-start(), calls=%async_computation.8 | async-start | bytes 3063808
  473.3 9.6 %collective-permute-start.20 = (f32[3,2048]{1,0:T(4,128)S(1)}, f32[3,2048]{1,0:T(4,128)S(1)}, u32[]{:S(2)}, u32[]{:S(2)}) collective-permute-start(f32[3,2048]{1,0:T(4,128)S(1)} %copy.598), channel_id=1, source_target_pairs={{2,0},{4,2},{6,4},{8,6},{10,8},{12,10},{14,12},{16,14},{18,16},{20... | collective-permute-start | bytes 73736 | tf_op jit(solution)/shard_map/ppermute | solution.py:19
  504.9 8.7 %collective-permute-start.27 = (bf16[8,64,3080]{2,1,0:T(8,128)(2,1)}, bf16[8,64,3080]{2,1,0:T(8,128)(2,1)}, u32[]{:S(2)}, u32[]{:S(2)}) collective-permute-start(bf16[8,64,3080]{2,1,0:T(8,128)(2,1)} %dynamic-slice_bitcast_fusion), channel_id=1, source_target_pairs={{0,2},{2,0},{4,6},{6,4},{8,10},{10,8},{12,14},{14,12},{16,18},{18,... | collective-permute-start | bytes 9461768 | tf_op jit(solution)/shard_map/ppermute | solution.py:253
  510.0 157.1 %reduce-scatter.8.cloned.1.call-start = ((), (), s32[]{:S(2)}) async-start(), calls=%async_computation.7 | async-start | bytes 6127616 | tf_op jit(solution)/shard_map/reduce_scatter | solution.py:283
  517.5 36.8 %copy-start.21 = (bf16[8,64,3080]{2,1,0:T(8,128)(2,1)}, bf16[8,64,3080]{2,1,0:T(8,128)(2,1)S(1)}, u32[]{:S(2)}) copy-start(bf16[8,64,3080]{2,1,0:T(8,128)(2,1)S(1)} %fusion) | copy-start | bytes 9461764
  518.3 10.3 %collective-permute-start.28 = (bf16[64,3080]{1,0:T(8,128)(2,1)}, bf16[64,3080]{1,0:T(8,128)(2,1)}, u32[]{:S(2)}, u32[]{:S(2)}) collective-permute-start(bf16[64,3080]{1,0:T(8,128)(2,1)} %dynamic-slice_bitcast_fusion.1), channel_id=1, source_target_pairs={{0,8},{8,16},{16,24},{24,28},{28,20},{20,12},{12,4},{4,0},{6,14},{... | collective-permute-start | bytes 1182728 | tf_op jit(solution)/shard_map/ppermute | solution.py:262
  530.5 9.0 %collective-permute-start.29 = (bf16[64,3080]{1,0:T(8,128)(2,1)}, bf16[64,3080]{1,0:T(8,128)(2,1)}, u32[]{:S(2)}, u32[]{:S(2)}) collective-permute-start(bf16[64,3080]{1,0:T(8,128)(2,1)} %fusion.57), channel_id=1, source_target_pairs={{0,8},{8,16},{16,24},{24,28},{28,20},{20,12},{12,4},{4,0},{6,14},{... | collective-permute-start | bytes 1182728 | tf_op jit(solution)/shard_map/ppermute | solution.py:262
  532.6 6.7 collective-permute-start.22
  540.9 13.3 %collective-permute-start.30 = (bf16[64,3080]{1,0:T(8,128)(2,1)S(1)}, bf16[64,3080]{1,0:T(8,128)(2,1)S(1)}, u32[]{:S(2)}, u32[]{:S(2)}) collective-permute-start(bf16[64,3080]{1,0:T(8,128)(2,1)S(1)} %fusion.56), channel_id=1, source_target_pairs={{0,8},{8,16},{16,24},{24,28},{28,20},{20,12},{12,4},{4,0},{6,14},{... | collective-permute-start | bytes 1182728 | tf_op jit(solution)/shard_map/ppermute | solution.py:262
  554.4 10.1 %collective-permute-start.31 = (bf16[64,3080]{1,0:T(8,128)(2,1)S(1)}, bf16[64,3080]{1,0:T(8,128)(2,1)S(1)}, u32[]{:S(2)}, u32[]{:S(2)}) collective-permute-start(bf16[64,3080]{1,0:T(8,128)(2,1)S(1)} %fusion.55), channel_id=1, source_target_pairs={{0,8},{8,16},{16,24},{24,28},{28,20},{20,12},{12,4},{4,0},{6,14},{... | collective-permute-start | bytes 1182728 | tf_op jit(solution)/shard_map/ppermute | solution.py:262
  559.7 14.1 %collective-permute-start.21 = (bf16[256,1024]{1,0:T(8,128)(2,1)S(1)}, bf16[256,1024]{1,0:T(8,128)(2,1)S(1)}, u32[]{:S(2)}, u32[]{:S(2)}) collective-permute-start(bf16[256,1024]{1,0:T(8,128)(2,1)S(1)} %convolution_convert_fusion.4), channel_id=1, source_target_pairs={{0,1},{1,0},{2,3},{3,2},{4,5},{5,4},{6,7},{7,6},{8,9},{9,8},{10,11... | collective-permute-start | bytes 1572872 | tf_op jit(solution)/shard_map/ppermute | solution.py:64
  565.6 22.9 %collective-permute-start.32 = (bf16[64,3080]{1,0:T(8,128)(2,1)S(1)}, bf16[64,3080]{1,0:T(8,128)(2,1)S(1)}, u32[]{:S(2)}, u32[]{:S(2)}) collective-permute-start(bf16[64,3080]{1,0:T(8,128)(2,1)S(1)} %fusion.54), channel_id=1, source_target_pairs={{0,8},{8,16},{16,24},{24,28},{28,20},{20,12},{12,4},{4,0},{6,14},{... | collective-permute-start | bytes 1182728 | tf_op jit(solution)/shard_map/ppermute | solution.py:262
  574.4 1.2 collective-permute-start.23
  575.6 6.4 collective-permute-start.24
  582.1 4.1 collective-permute-start.25
  586.2 6.8 %collective-permute-start.26 = (f32[10504]{0:T(1024)S(1)}, f32[10504]{0:T(1024)S(1)}, u32[]{:S(2)}, u32[]{:S(2)}) collective-permute-start(f32[10504]{0:T(1024)S(1)} %add.631), channel_id=1, source_target_pairs={{0,16},{2,18},{4,20},{6,22},{8,24},{10,26},{12,28},{14,30},{16,0},... | collective-permute-start | bytes 126056 | tf_op jit(solution)/shard_map/ppermute | solution.py:276
  589.6 8.0 %collective-permute-start.33 = (bf16[64,3080]{1,0:T(8,128)(2,1)S(1)}, bf16[64,3080]{1,0:T(8,128)(2,1)S(1)}, u32[]{:S(2)}, u32[]{:S(2)}) collective-permute-start(bf16[64,3080]{1,0:T(8,128)(2,1)S(1)} %fusion.53), channel_id=1, source_target_pairs={{0,8},{8,16},{16,24},{24,28},{28,20},{20,12},{12,4},{4,0},{6,14},{... | collective-permute-start | bytes 1182728 | tf_op jit(solution)/shard_map/ppermute | solution.py:262
  598.7 8.8 %collective-permute-start.34 = (bf16[64,3080]{1,0:T(8,128)(2,1)S(1)}, bf16[64,3080]{1,0:T(8,128)(2,1)S(1)}, u32[]{:S(2)}, u32[]{:S(2)}) collective-permute-start(bf16[64,3080]{1,0:T(8,128)(2,1)S(1)} %fusion.52), channel_id=1, source_target_pairs={{0,8},{8,16},{16,24},{24,28},{28,20},{20,12},{12,4},{4,0},{6,14},{... | collective-permute-start | bytes 1182728 | tf_op jit(solution)/shard_map/ppermute | solution.py:262
  (174 other events, 1121.6 us)
Sparse Core Ops, SparseCore 0:
  10.2 44.9 all-gather.3
  58.1 64.6 all-gather.5
  125.0 49.8 all-gather.7
  392.5 67.3 reduce-scatter.5
  510.1 72.5 reduce-scatter.9
  586.4 80.5 reduce-scatter.7

commit v3 on v1

--- a/solution.py
+++ b/solution.py
@@ -202,8 +202,22 @@
     )
 
 
+def doubled_sum(values, axis):
+    size = lax.axis_size(axis)
+    if size & (size - 1):
+        return lax.psum(values, axis)
+    distance = 1
+    while distance < size:
+        values = values + lax.ppermute(values, axis, [(i, i ^ distance) for i in range(size)])
+        distance = 2 * distance
+    return values
+
+
 def summed_rows(left, right):
-    part = contract_rows(left, right).astype(jnp.bfloat16)
+    return summed_part(contract_rows(left, right).astype(jnp.bfloat16))
+
+
+def summed_part(part):
     share = lax.psum_scatter(part, "dp", scatter_dimension=0, tiled=True)
     return share.astype(jnp.float32)
 
@@ -333,14 +347,19 @@
     output = (residual + mlp_total).astype(jnp.bfloat16)
     grad_out = cotangent.astype(jnp.float32)
     grad_hidden = jnp.dot(cotangent, full_down, preferred_element_type=jnp.float32)
-    share_down = summed_rows(cotangent, hidden)
+    part_down = contract_rows(cotangent, hidden).astype(jnp.bfloat16)
     sigma_two = jax.nn.sigmoid(gate_two)
     grad_gate_two = grad_hidden * up_two * sigma_two * (1.0 + gate_two * (1.0 - sigma_two))
     grad_up_two = grad_hidden * gate_two * sigma_two
     grad_gu_low = jnp.concatenate([grad_gate_two, grad_up_two], axis=1).astype(jnp.bfloat16)
-    share_gu = summed_rows(normed_two, grad_gu_low)
+    part_gu = contract_rows(normed_two, grad_gu_low).astype(jnp.bfloat16)
     grad_normed_two_part = contract_cols(grad_gu_low, matrix_gu)
     grad_normed_two = pair_sum(grad_normed_two_part.astype(jnp.bfloat16), "tensor")
+    grad_normed_two, part_down, part_gu = lax.optimization_barrier(
+        (grad_normed_two, part_down, part_gu)
+    )
+    share_down = summed_part(part_down)
+    share_gu = summed_part(part_gu)
     gain_two_grad = jnp.sum(grad_normed_two * unit_two, axis=0)
     grad_residual = grad_out + norm_back(grad_normed_two * gains[1], unit_two, scale_two)
     grad_res_low = grad_residual.astype(jnp.bfloat16)
@@ -405,7 +424,7 @@
         grad_decay_log,
         grad_decay_bias,
     )
-    small = lax.psum(jnp.concatenate(small_parts), "dp")
+    small = doubled_sum(jnp.concatenate(small_parts), "dp")
     sums = []
     at = 0
     for part in small_parts:

time: 609 us -> 612 us (level)
  blocking collectives: 58.4 us -> 0 us
  waiting for transfers between devices: 190 us -> 220 us
  local copies, waits for them, and re-layouts: 109 us -> 128 us
  starting transfers between devices: 63.5 us -> 71.7 us
    psum x1 -> x0, blocking collectives: 58.4 us -> none  [local(): small = lax.psum(jnp.concatenate(small_parts), 'dp')]
    reduce_scatter x3, waiting for transfers between devices: 40.7 us -> 77.3 us  [summed_part(): share = lax.psum_scatter(part, 'dp', scatter_dimension=0, tiled=True)]
    ppermute x5, waiting for transfers between devices: 49.1 us -> 32.7 us  [pair_sum(): other = lax.ppermute(part, axis, [(0, 1), (1, 0)])]
    squeeze x2, local copies, waits for them, and re-layouts: 2.97 us -> 15 us  [local(): maps = [jnp.concatenate([kept_a[0], step_b[0]], axis=-1)]]
    ppermute x0 -> x4, waiting for transfers between devices: none -> 9.1 us  [doubled_sum(): lax.ppermute(values, axis, [(i, i ^ distance) for i in range(size)])]
    ppermute x0 -> x4, starting transfers between devices: none -> 6.65 us  [doubled_sum(): lax.ppermute(values, axis, [(i, i ^ distance) for i in range(size)])]
    unnamed x345 -> x367, local copies, waits for them, and re-layouts: 27.6 us -> 33 us
  transfers between devices with their start and end apart: 23 -> 27, of which waited for: 15 -> 19; matrix products, arithmetic and copies ran while one was open for 40% -> 42% of each run, Pallas kernels for 0% -> 0%
where the time goes in v3:
time: 612 us; the launch traced here: 604 us
  waiting for transfers between devices  220 us (36%)
  local copies, waits for them, and re-layouts  128 us (21%)
  matrix products  91.9 us (15%)
  other arithmetic  75.2 us (12%)
  starting transfers between devices  71.7 us (12%)
  between operations  17.1 us (3%)
    reduce_scatter x3, waiting for transfers between devices, summed_part(): share = lax.psum_scatter(part, 'dp', scatter_dimension=0, tiled=True)  77.3 us
    all_gather x1, waiting for transfers between devices, local(): lax.all_gather(jnp.concatenate([query_key_weight.reshape(-1, 2 * width_k)...  58.6 us
    ppermute x10, starting transfers between devices, shifted(): return lax.ppermute(block, axis, route)  56.4 us
    ppermute x10, waiting for transfers between devices, shifted(): return lax.ppermute(block, axis, route)  41 us
    unnamed x367, local copies, waits for them, and re-layouts  33 us
    ppermute x5, waiting for transfers between devices, pair_sum(): other = lax.ppermute(part, axis, [(0, 1), (1, 0)])  32.7 us
    dot_general x27, matrix products, matmul(): return jnp.einsum('...ij,...jk->...ik', left, right, precision=accuracy)  22.4 us
    reshape x6, local copies, waits for them, and re-layouts, from_blocks(): blocked.transpose(0, 2, 1, 3)  16.2 us
  transfers between devices with their start and end apart: 27, of which 19 were waited for; matrix products, arithmetic and copies ran while one was open for 42% of the time, Pallas kernels for 0%

profile of v3, /device:TPU:0, one launch (start us, length us, event | category | flops | bytes accessed | tf_op | source)
XLA Modules:
  0.0 604.3 jit_solution(13817617299303650594)
XLA Ops:
  18.5 58.6 %all-gather.5.cloned.1.call-done = bf16[1024,3080]{1,0:T(8,128)(2,1)} async-done(((bf16[64,3080]{1,0:T(8,128)(2,1)}), bf16[1024,3080]{1,0:T(8,128)(2,1)}) %all-gather.5.cloned.1.call-update) | async-done | bytes 6307856 | tf_op jit(solution)/shard_map/all_gather | solution.py:269
  77.2 5.7 fusion.227
  85.4 3.0 collective-permute-start
  94.4 4.2 fusion.6
  124.3 2.6 copy.555
  129.4 13.2 %slice_bitcast_fusion.15 = f32[4,128,128]{1,2,0:T(8,128)} fusion(f32[4,4,128,128]{2,3,1,0:T(8,128)S(1)} %subtract_multiply_fusion.2), kind=kLoop, calls=%fused_computation.230 | loop fusion | bytes 524288 | tf_op jit(solution)/shard_map/squeeze | solution.py:312
  147.5 3.8 collective-permute-start.1
  152.6 16.2 %collective-permute-start.2 = (bf16[4,128,384]{2,1,0:T(8,128)(2,1)S(1)}, bf16[4,128,384]{2,1,0:T(8,128)(2,1)S(1)}, u32[]{:S(2)}, u32[]{:S(2)}) collective-permute-start(bf16[4,128,384]{2,1,0:T(8,128)(2,1)S(1)} %collective-permute-done.1), channel_id=1, source_target_pairs={{0,2},{2,4},{4,6},{6,8},{8,10},{10,12},{12,14},{14,16},{16,18},{18... | collective-permute-start | bytes 1179656 | tf_op jit(solution)/shard_map/ppermute | solution.py:19
  171.5 10.8 %collective-permute-start.3 = (bf16[4,128,384]{2,1,0:T(8,128)(2,1)}, bf16[4,128,384]{2,1,0:T(8,128)(2,1)}, u32[]{:S(2)}, u32[]{:S(2)}) collective-permute-start(bf16[4,128,384]{2,1,0:T(8,128)(2,1)} %get-tuple-element.206), channel_id=1, source_target_pairs={{0,4},{2,6},{4,8},{6,10},{8,12},{10,14},{12,16},{14,18},{16,20},{1... | collective-permute-start | bytes 1179656 | tf_op jit(solution)/shard_map/ppermute | solution.py:19
  188.6 15.7 %collective-permute-start.4 = (bf16[4,128,256]{2,1,0:T(8,128)(2,1)S(1)}, bf16[4,128,256]{2,1,0:T(8,128)(2,1)S(1)}, u32[]{:S(2)}, u32[]{:S(2)}) collective-permute-start(bf16[4,128,256]{2,1,0:T(8,128)(2,1)S(1)} %slice.544), channel_id=1, source_target_pairs={{0,8},{2,10},{4,12},{6,14},{8,16},{10,18},{12,20},{14,22},{16,24},... | collective-permute-start | bytes 786440 | tf_op jit(solution)/shard_map/ppermute | solution.py:19
  204.8 4.3 collective-permute-done.4
  216.3 2.8 copy.542
  219.1 3.2 reshape.409
  222.3 2.7 multiply_convert_fusion.4
  225.1 2.6 convolution_convert_fusion.6
  229.2 10.0 %collective-permute-done.5 = bf16[256,1024]{1,0:T(8,128)(2,1)S(1)} collective-permute-done((bf16[256,1024]{1,0:T(8,128)(2,1)S(1)}, bf16[256,1024]{1,0:T(8,128)(2,1)S(1)}, u32[]{:S(2)}, u32[]{:S(2)}) %collective-permute-start.5) | collective-permute-done | bytes 524320 | tf_op jit(solution)/shard_map/ppermute | solution.py:64
  241.0 6.3 %fusion.210 = f32[256,2816]{1,0:T(8,128)} fusion(bf16[1024,2816]{1,0:T(8,128)(2,1)} %all-gather.9.cloned.1.call-done, f32[256,1024]{1,0:T(8,128)} %get-tuple-element.138, f32[1024]{0:T(1024)S(1)} %bitcast.318, f32[256]{0:T(256)} %add_rsqrt_fusion.2), kind=kOutput, calls=%fused_computation.426 | convolution fusion | flops 1477181440 | bytes 9704448 | tf_op jit(solution)/shard_map/dot_general | solution.py:342
  247.3 4.3 multiply_convert_fusion.1
  260.7 4.3 convolution_convert_fusion.1
  265.0 4.5 collective-permute-done.7
  271.8 4.6 collective-permute-done.6
  285.9 3.3 fusion.112
  289.2 2.7 reshape.382
  294.4 3.5 fusion.42
  297.9 3.1 reshape.415
  301.0 2.7 copy.474
  303.8 4.6 copy.547
  309.1 3.3 multiply_reduce_fusion.4
  324.7 8.5 %collective-permute-done.9 = bf16[4,128,384]{2,1,0:T(8,128)(2,1)S(1)} collective-permute-done((bf16[4,128,384]{2,1,0:T(8,128)(2,1)S(1)}, bf16[4,128,384]{2,1,0:T(8,128)(2,1)S(1)}, u32[]{:S(2)}, u32[]{:S(2)}) %collective-permute-start.9) | collective-permute-done | bytes 393248 | tf_op jit(solution)/shard_map/ppermute | solution.py:19
  336.8 11.4 %collective-permute-done.10 = bf16[4,128,384]{2,1,0:T(8,128)(2,1)S(1)} collective-permute-done((bf16[4,128,384]{2,1,0:T(8,128)(2,1)S(1)}, bf16[4,128,384]{2,1,0:T(8,128)(2,1)S(1)}, u32[]{:S(2)}, u32[]{:S(2)}) %collective-permute-start.10) | collective-permute-done | bytes 393248 | tf_op jit(solution)/shard_map/ppermute | solution.py:19
  355.5 10.4 %collective-permute-done.11 = bf16[4,128,256]{2,1,0:T(8,128)(2,1)} collective-permute-done((bf16[4,128,256]{2,1,0:T(8,128)(2,1)}, bf16[4,128,256]{2,1,0:T(8,128)(2,1)}, u32[]{:S(2)}, u32[]{:S(2)}) %collective-permute-start.11) | collective-permute-done | bytes 262176 | tf_op jit(solution)/shard_map/ppermute | solution.py:19
  387.0 5.6 multiply_reduce_fusion.13
  398.4 2.6 copy.494
  417.5 2.7 multiply_bitcast_fusion
  420.6 2.6 reshape.412
  423.2 2.8 reshape.411
  426.1 2.8 copy.544
  428.9 3.3 reshape.410
  437.1 3.6 multiply_reduce_fusion.3
  448.5 7.4 %pad_add_fusion = f32[259,2048]{0,1:T(8,128)} fusion(f32[256,2048]{0,1:T(8,128)} %copy-done.11, f32[256,2048]{0,1:T(8,128)} %copy-done.12, f32[256,2048]{0,1:T(8,128)} %copy-done.13, f32[256,2048]{0,1:T(8,128)S(1)} %get-tuple-element.153), kind=kLoop, calls=%fused_computation.4 | loop fusion | flops 1591296 | bytes 10510336 | tf_op jit(solution)/shard_map/transpose(jvp())/add_any | solution.py:170
  456.3 2.7 fusion.5
  459.1 4.9 convolution_convert_fusion
  468.4 5.0 convolution_convert_fusion.4
  475.6 12.1 %collective-permute-done.13 = bf16[256,1024]{1,0:T(8,128)(2,1)S(1)} collective-permute-done((bf16[256,1024]{1,0:T(8,128)(2,1)S(1)}, bf16[256,1024]{1,0:T(8,128)(2,1)S(1)}, u32[]{:S(2)}, u32[]{:S(2)}) %collective-permute-start.13) | collective-permute-done | bytes 524320 | tf_op jit(solution)/shard_map/ppermute | solution.py:64
  490.0 3.6 collective-permute-done.16
  493.6 4.0 collective-permute-start.17
  497.6 2.7 collective-permute-done.17
  514.3 77.3 %reduce-scatter.7.cloned.1.call-done = bf16[64,3080]{1,0:T(8,128)(2,1)} async-done(((bf16[1024,3080]{1,0:T(8,128)(2,1)}), bf16[64,3080]{1,0:T(8,128)(2,1)}) %reduce-scatter.7.cloned.1.call-update) | async-done | bytes 394256 | tf_op jit(solution)/shard_map/reduce_scatter | solution.py:221
  (608 shorter events, 204.5 us)
Async XLA Ops:
  7.3 69.9 %all-gather.5.cloned.1.call-start = ((), (), s32[]{:S(2)}) async-start(), calls=%async_computation.4 | async-start | bytes 6963200 | tf_op jit(solution)/shard_map/all_gather | solution.py:269
  10.9 214.2 %all-gather.7.cloned.1.call-start = ((), (), s32[]{:S(2)}) async-start(), calls=%async_computation.5 | async-start | bytes 2228224 | tf_op jit(solution)/shard_map/all_gather | solution.py:282
  11.7 229.4 %all-gather.9.cloned.1.call-start = ((), (), s32[]{:S(2)}) async-start(), calls=%async_computation.6 | async-start | bytes 6127616 | tf_op jit(solution)/shard_map/all_gather | solution.py:338
  12.5 234.8 %all-gather.11.cloned.1.call-start = ((), (), s32[]{:S(2)}) async-start(), calls=%async_computation.7 | async-start | bytes 3063808 | tf_op jit(solution)/shard_map/all_gather | solution.py:341
  13.1 495.3 %reduce-scatter.9.cloned.1.call-start = ((), (), s32[]{:S(2)}) async-start(), calls=%async_computation.9 | async-start | bytes 2228224 | tf_op jit(solution)/shard_map/reduce_scatter | solution.py:221
  15.1 67.7 %copy-start.169 = (f32[4]{0:T(128)}, f32[4]{0:T(128)S(1)}, u32[]{:S(2)}) copy-start(f32[4]{0:T(128)S(1)} %exponential_negate_fusion) | copy-start | bytes 52
  16.4 66.4 %copy-start.154 = (f32[256]{0:T(256)}, f32[256]{0:T(256)S(1)}, u32[]{:S(2)}) copy-start(f32[256]{0:T(256)S(1)} %add_rsqrt_fusion.3) | copy-start | bytes 3076
  17.0 65.8 %copy-start.120 = (f32[1,1024]{1,0:T(1,128)}, f32[1,1024]{1,0:T(1,128)S(1)}, u32[]{:S(2)}) copy-start(f32[1,1024]{1,0:T(1,128)S(1)} %get-tuple-element.193) | copy-start | bytes 12292
  85.4 6.8 %collective-permute-start = (bf16[3,2048]{0,1:T(8,128)(2,1)S(1)}, bf16[3,2048]{0,1:T(8,128)(2,1)}, u32[]{:S(2)}, u32[]{:S(2)}) collective-permute-start(bf16[3,2048]{0,1:T(8,128)(2,1)S(1)} %slice.342), channel_id=1, source_target_pairs={{0,2},{2,4},{4,6},{6,8},{8,10},{10,12},{12,14},{14,16},{16,18},{18... | collective-permute-start | bytes 36872 | tf_op jit(solution)/shard_map/ppermute | solution.py:19
  89.2 37.7 %copy-start.140 = (f32[4,4]{1,0:T(4,128)}, f32[4,4]{1,0:T(4,128)S(1)}, u32[]{:S(2)}) copy-start(f32[4,4]{1,0:T(4,128)S(1)} %fusion.209) | copy-start | bytes 196
  146.9 24.5 %copy-start.33 = (f32[4,128,384]{2,1,0:T(8,128)}, f32[4,128,384]{2,1,0:T(8,128)S(1)}, u32[]{:S(2)}) copy-start(f32[4,128,384]{2,1,0:T(8,128)S(1)} %convolution_add_fusion.7) | copy-start | bytes 2359300
  147.0 35.3 %copy-start.174 = (bf16[256]{0:T(256)(128)(2,1)S(1)}, bf16[256]{0:T(256)(128)(2,1)}, u32[]{:S(2)}) copy-start(bf16[256]{0:T(256)(128)(2,1)} %param.26) | copy-start | bytes 1540
  147.5 5.1 collective-permute-start.1
  152.6 17.6 %collective-permute-start.2 = (bf16[4,128,384]{2,1,0:T(8,128)(2,1)S(1)}, bf16[4,128,384]{2,1,0:T(8,128)(2,1)S(1)}, u32[]{:S(2)}, u32[]{:S(2)}) collective-permute-start(bf16[4,128,384]{2,1,0:T(8,128)(2,1)S(1)} %collective-permute-done.1), channel_id=1, source_target_pairs={{0,2},{2,4},{4,6},{6,8},{8,10},{10,12},{12,14},{14,16},{16,18},{18... | collective-permute-start | bytes 1179656 | tf_op jit(solution)/shard_map/ppermute | solution.py:19
  171.5 15.7 %collective-permute-start.3 = (bf16[4,128,384]{2,1,0:T(8,128)(2,1)}, bf16[4,128,384]{2,1,0:T(8,128)(2,1)}, u32[]{:S(2)}, u32[]{:S(2)}) collective-permute-start(bf16[4,128,384]{2,1,0:T(8,128)(2,1)} %get-tuple-element.206), channel_id=1, source_target_pairs={{0,4},{2,6},{4,8},{6,10},{8,12},{10,14},{12,16},{14,18},{16,20},{1... | collective-permute-start | bytes 1179656 | tf_op jit(solution)/shard_map/ppermute | solution.py:19
  184.5 19.9 %copy-start.57 = (f32[4,128,256]{2,1,0:T(8,128)S(1)}, f32[4,128,256]{2,1,0:T(8,128)}, u32[]{:S(2)}) copy-start(f32[4,128,256]{2,1,0:T(8,128)} %get-tuple-element.151) | copy-start | bytes 1572868
  184.5 19.9 %copy-start.80 = (f32[4,128,128]{2,1,0:T(8,128)S(1)}, f32[4,128,128]{2,1,0:T(8,128)}, u32[]{:S(2)}) copy-start(f32[4,128,128]{2,1,0:T(8,128)} %copy.462) | copy-start | bytes 786436
  185.6 18.8 %copy-start.1 = (f32[4,4,64,384]{3,2,1,0:T(8,128)S(1)}, f32[4,4,64,384]{3,2,1,0:T(8,128)}, u32[]{:S(2)}) copy-start(f32[4,4,64,384]{3,2,1,0:T(8,128)} %copy-done) | copy-start | bytes 4718596
  185.6 18.9 %copy-start.68 = (bf16[256,4,128]{2,0,1:T(8,128)(2,1)S(1)}, bf16[256,4,128]{2,0,1:T(8,128)(2,1)}, u32[]{:S(2)}) copy-start(bf16[256,4,128]{2,0,1:T(8,128)(2,1)} %copy-done.67) | copy-start | bytes 786436
  185.7 18.9 %copy-start.108 = (f32[4,4,64]{2,1,0:T(4,128)S(1)}, f32[4,4,64]{2,1,0:T(4,128)}, u32[]{:S(2)}) copy-start(f32[4,4,64]{2,1,0:T(4,128)} %copy.457) | copy-start | bytes 12292
  188.6 20.8 %copy-start.32 = (f32[4,128,384]{2,1,0:T(8,128)S(1)}, f32[4,128,384]{2,1,0:T(8,128)}, u32[]{:S(2)}) copy-start(f32[4,128,384]{2,1,0:T(8,128)} %copy-done.31) | copy-start | bytes 2359300
  188.6 20.8 %copy-start.34 = (f32[4,128,384]{2,1,0:T(8,128)S(1)}, f32[4,128,384]{2,1,0:T(8,128)}, u32[]{:S(2)}) copy-start(f32[4,128,384]{2,1,0:T(8,128)} %copy-done.33) | copy-start | bytes 2359300
  188.6 20.4 %collective-permute-start.4 = (bf16[4,128,256]{2,1,0:T(8,128)(2,1)S(1)}, bf16[4,128,256]{2,1,0:T(8,128)(2,1)S(1)}, u32[]{:S(2)}, u32[]{:S(2)}) collective-permute-start(bf16[4,128,256]{2,1,0:T(8,128)(2,1)S(1)} %slice.544), channel_id=1, source_target_pairs={{0,8},{2,10},{4,12},{6,14},{8,16},{10,18},{12,20},{14,22},{16,24},... | collective-permute-start | bytes 786440 | tf_op jit(solution)/shard_map/ppermute | solution.py:19
  227.7 11.6 %collective-permute-start.5 = (bf16[256,1024]{1,0:T(8,128)(2,1)S(1)}, bf16[256,1024]{1,0:T(8,128)(2,1)S(1)}, u32[]{:S(2)}, u32[]{:S(2)}) collective-permute-start(bf16[256,1024]{1,0:T(8,128)(2,1)S(1)} %convolution_convert_fusion.6), channel_id=1, source_target_pairs={{0,1},{1,0},{2,3},{3,2},{4,5},{5,4},{6,7},{7,6},{8,9},{9,8},{10,11... | collective-permute-start | bytes 1572872 | tf_op jit(solution)/shard_map/ppermute | solution.py:64
  254.3 15.2 %collective-permute-start.7 = (bf16[256,1024]{1,0:T(8,128)(2,1)}, bf16[256,1024]{1,0:T(8,128)(2,1)}, u32[]{:S(2)}, u32[]{:S(2)}) collective-permute-start(bf16[256,1024]{1,0:T(8,128)(2,1)} %convolution_convert_fusion.7), channel_id=1, source_target_pairs={{0,1},{1,0},{2,3},{3,2},{4,5},{5,4},{6,7},{7,6},{8,9},{9,8},{10,11... | collective-permute-start | bytes 1572872 | tf_op jit(solution)/shard_map/ppermute | solution.py:64
  260.2 16.2 %collective-permute-start.6 = (bf16[256,1024]{1,0:T(8,128)(2,1)}, bf16[256,1024]{1,0:T(8,128)(2,1)}, u32[]{:S(2)}, u32[]{:S(2)}) collective-permute-start(bf16[256,1024]{1,0:T(8,128)(2,1)} %convolution_convert_fusion.5), channel_id=1, source_target_pairs={{0,1},{1,0},{2,3},{3,2},{4,5},{5,4},{6,7},{7,6},{8,9},{9,8},{10,11... | collective-permute-start | bytes 1572872 | tf_op jit(solution)/shard_map/ppermute | solution.py:64
  282.0 227.9 %reduce-scatter.13.cloned.1.call-start = ((), (), s32[]{:S(2)}) async-start(), calls=%async_computation.11 | async-start | bytes 3063808
  308.4 203.6 %reduce-scatter.11.cloned.1.call-start = ((), (), s32[]{:S(2)}) async-start(), calls=%async_computation.10 | async-start | bytes 6127616 | tf_op jit(solution)/shard_map/reduce_scatter | solution.py:221
  313.5 37.4 %copy-start.3 = (f32[4,4,64,256]{3,2,1,0:T(8,128)}, f32[4,4,64,256]{3,2,1,0:T(8,128)S(1)}, u32[]{:S(2)}) copy-start(f32[4,4,64,256]{3,2,1,0:T(8,128)S(1)} %fusion.39) | copy-start | bytes 3145732
  319.1 14.3 %copy-start.29 = (f32[4,128,384]{2,1,0:T(8,128)}, f32[4,128,384]{2,1,0:T(8,128)S(1)}, u32[]{:S(2)}) copy-start(f32[4,128,384]{2,1,0:T(8,128)S(1)} %convolution_add_fusion.3) | copy-start | bytes 2359300
  319.1 15.6 %copy-start.69 = (bf16[256,4,128]{2,0,1:T(8,128)(2,1)S(1)}, bf16[256,4,128]{2,0,1:T(8,128)(2,1)}, u32[]{:S(2)}) copy-start(bf16[256,4,128]{2,0,1:T(8,128)(2,1)} %copy-done.67) | copy-start | bytes 786436
  319.7 16.0 %copy-start.49 = (bf16[256,4,256]{2,0,1:T(8,128)(2,1)S(1)}, bf16[256,4,256]{2,0,1:T(8,128)(2,1)}, u32[]{:S(2)}) copy-start(bf16[256,4,256]{2,0,1:T(8,128)(2,1)} %copy.454) | copy-start | bytes 1572868
  319.7 3.7 collective-permute-start.8
  323.4 9.8 %collective-permute-start.9 = (bf16[4,128,384]{2,1,0:T(8,128)(2,1)S(1)}, bf16[4,128,384]{2,1,0:T(8,128)(2,1)S(1)}, u32[]{:S(2)}, u32[]{:S(2)}) collective-permute-start(bf16[4,128,384]{2,1,0:T(8,128)(2,1)S(1)} %collective-permute-done.8), channel_id=1, source_target_pairs={{2,0},{4,2},{6,4},{8,6},{10,8},{12,10},{14,12},{16,14},{18,16},{20... | collective-permute-start | bytes 1179656 | tf_op jit(solution)/shard_map/ppermute | solution.py:19
  333.5 14.8 %collective-permute-start.10 = (bf16[4,128,384]{2,1,0:T(8,128)(2,1)S(1)}, bf16[4,128,384]{2,1,0:T(8,128)(2,1)S(1)}, u32[]{:S(2)}, u32[]{:S(2)}) collective-permute-start(bf16[4,128,384]{2,1,0:T(8,128)(2,1)S(1)} %get-tuple-element.212), channel_id=1, source_target_pairs={{4,0},{6,2},{8,4},{10,6},{12,8},{14,10},{16,12},{18,14},{20,16},{2... | collective-permute-start | bytes 1179656 | tf_op jit(solution)/shard_map/ppermute | solution.py:19
  349.6 16.3 %collective-permute-start.11 = (bf16[4,128,256]{2,1,0:T(8,128)(2,1)}, bf16[4,128,256]{2,1,0:T(8,128)(2,1)}, u32[]{:S(2)}, u32[]{:S(2)}) collective-permute-start(bf16[4,128,256]{2,1,0:T(8,128)(2,1)} %slice.543), channel_id=1, source_target_pairs={{8,0},{10,2},{12,4},{14,6},{16,8},{18,10},{20,12},{22,14},{24,16},... | collective-permute-start | bytes 786440 | tf_op jit(solution)/shard_map/ppermute | solution.py:19
  354.0 237.6 %reduce-scatter.7.cloned.1.call-start = ((), (), s32[]{:S(2)}) async-start(), calls=%async_computation.8 | async-start | bytes 6963200 | tf_op jit(solution)/shard_map/reduce_scatter | solution.py:221
  396.1 14.8 %copy-start.134 = (f32[4,4]{1,0:T(4,128)S(1)}, f32[4,4]{1,0:T(4,128)}, u32[]{:S(2)}) copy-start(f32[4,4]{1,0:T(4,128)} %copy-done.133) | copy-start | bytes 196
  401.0 16.5 %copy-start.103 = (f32[4,4,64]{2,1,0:T(4,128)S(1)}, f32[4,4,64]{2,1,0:T(4,128)}, u32[]{:S(2)}) copy-start(f32[4,4,64]{2,1,0:T(4,128)} %copy.425) | copy-start | bytes 12292
  445.9 9.9 %collective-permute-start.12 = (f32[3,2048]{1,0:T(4,128)S(1)}, f32[3,2048]{1,0:T(4,128)S(1)}, u32[]{:S(2)}, u32[]{:S(2)}) collective-permute-start(f32[3,2048]{1,0:T(4,128)S(1)} %copy.491), channel_id=1, source_target_pairs={{2,0},{4,2},{6,4},{8,6},{10,8},{12,10},{14,12},{16,14},{18,16},{20... | collective-permute-start | bytes 73736 | tf_op jit(solution)/shard_map/ppermute | solution.py:19
  464.7 3.8 collective-permute-start.14
  468.4 19.7 %copy-start.152 = (f32[1024]{0:T(1024)S(1)}, f32[1024]{0:T(1024)}, u32[]{:S(2)}) copy-start(f32[1024]{0:T(1024)} %get-tuple-element.124) | copy-start | bytes 12292
  473.5 28.9 %copy-start.18 = (f32[256,1024]{1,0:T(8,128)S(1)}, f32[256,1024]{1,0:T(8,128)}, u32[]{:S(2)}) copy-start(f32[256,1024]{1,0:T(8,128)} %copy-done.16) | copy-start | bytes 3145732
  473.5 14.2 %collective-permute-start.13 = (bf16[256,1024]{1,0:T(8,128)(2,1)S(1)}, bf16[256,1024]{1,0:T(8,128)(2,1)S(1)}, u32[]{:S(2)}, u32[]{:S(2)}) collective-permute-start(bf16[256,1024]{1,0:T(8,128)(2,1)S(1)} %convolution_convert_fusion.4), channel_id=1, source_target_pairs={{0,1},{1,0},{2,3},{3,2},{4,5},{5,4},{6,7},{7,6},{8,9},{9,8},{10,11... | collective-permute-start | bytes 1572872 | tf_op jit(solution)/shard_map/ppermute | solution.py:64
  488.2 1.2 collective-permute-start.15
  489.5 4.1 collective-permute-start.16
  493.6 6.8 %collective-permute-start.17 = (f32[10504]{0:T(1024)S(1)}, f32[10504]{0:T(1024)S(1)}, u32[]{:S(2)}, u32[]{:S(2)}) collective-permute-start(f32[10504]{0:T(1024)S(1)} %add.376), channel_id=1, source_target_pairs={{0,8},{2,10},{4,12},{6,14},{8,0},{10,2},{12,4},{14,6},{16,24},{18,... | collective-permute-start | bytes 126056 | tf_op jit(solution)/shard_map/ppermute | solution.py:211
  500.3 5.0 collective-permute-start.18
  (156 other events, 549.4 us)
Sparse Core Ops, SparseCore 0:
  11.0 66.0 all-gather.4
  79.3 40.5 all-gather.6
  122.8 62.0 all-gather.8
  187.0 44.7 all-gather.10
  282.2 65.8 reduce-scatter.8
  352.2 63.8 reduce-scatter.12
  419.9 81.1 reduce-scatter.10
  505.1 86.4 reduce-scatter.6
